TPU v7x, 256 devices: a whole 4x4x8 slice. The times are simulated.
256 devices in a mesh: ha: 8 (over y, x_lo), wa: 32 (over x_hi, z, core).
Axes of the slice: x: 4 (x_hi: 2, x_lo: 2; x = x_hi * 2 + x_lo), y: 4, z: 8, core: 2. Of those that a mesh axis runs over, the one named last changes fastest.
Arguments:
- query_field: float32 [2, 128, 128, 256], P(None, 'ha', 'wa'), may hold values from -150 to 150, as said below
- key_field: float32 [2, 128, 128, 256], P(None, 'ha', 'wa'), may hold values from -6 to 6
- value_field: float32 [2, 128, 128, 256], P(None, 'ha', 'wa'), may hold values from -6 to 6
- output_grad: float32 [2, 128, 128, 256], P(None, 'ha', 'wa'), may hold values from -6 to 6
Outputs:
- query_grad: float32 [2, 128, 128, 256], P(None, 'ha', 'wa')
- key_grad: float32 [2, 128, 128, 256], P(None, 'ha', 'wa')
- value_grad: float32 [2, 128, 128, 256], P(None, 'ha', 'wa')
Inputs may be any that keep to these rules, and one draw needn't show every extreme that they name: `query_field`: queries and keys are real-valued with no structure promised.
All inputs are finite; a program needn't handle non-finite values.
Results may differ from a plain program's by a relative error of at most 0.0003.
Values sent between devices are 32-bit elements; how exact they have to be, the bound alone decides.
A program may use at most 128 MiB of HBM per device.

v0:
```python
import jax
import jax.numpy as jnp
from jax import lax
from jax.sharding import PartitionSpec as P

HEADS = 2
HEAD_DIM = 128
TILE = 16


def passed_along(block, axis, distance):
    devices = range(lax.axis_size(axis))
    route = [(i - distance, i) for i in devices if i - distance in devices]
    return lax.ppermute(block, axis, route)


def extended_2(value, sides, width):
    for axis, dim in sides:
        devices, length = (lax.axis_size(axis), value.shape[dim])
        up = [(i, (i + 1) % devices) for i in range(devices - 1)]
        down = [(j, i) for i, j in up]
        last = lax.slice_in_dim(value, length - width, length, axis=dim)
        first = lax.slice_in_dim(value, 0, width, axis=dim)
        before = lax.ppermute(last, axis, up)
        after = lax.ppermute(first, axis, down)
        value = jnp.concatenate([before, value, after], axis=dim)
    return value


def tile_grads(query_rows, grad_rows, key_rows, value_rows, key_valid):
    score_scale = HEAD_DIM ** (-0.5)
    highest = lax.Precision.HIGHEST
    mask_bias = jnp.where(key_valid, jnp.float32(0.0), jnp.float32(-1e30))
    query_parts = []
    key_parts = []
    value_parts = []
    for head_index in range(HEADS):
        head_start = head_index * HEAD_DIM
        head_stop = head_start + HEAD_DIM
        query_scaled = query_rows[:, head_start:head_stop] * score_scale
        grad_head = grad_rows[:, head_start:head_stop]
        key_head = key_rows[:, head_start:head_stop]
        value_head = value_rows[:, head_start:head_stop]
        scores = jnp.dot(query_scaled, key_head.T, precision=highest) + mask_bias[None, :]
        row_peak = jnp.max(scores, axis=1, keepdims=True)
        weights = jnp.exp(scores - row_peak)
        inverse = 1.0 / jnp.sum(weights, axis=1, keepdims=True)
        probabilities = weights * inverse
        dprobs = jnp.dot(grad_head, value_head.T, precision=highest)
        center = jnp.sum(probabilities * dprobs, axis=1, keepdims=True)
        dscores = probabilities * (dprobs - center)
        query_parts.append(jnp.dot(dscores, key_head, precision=highest) * score_scale)
        key_parts.append(jnp.dot(dscores.T, query_scaled, precision=highest))
        value_parts.append(jnp.dot(probabilities.T, grad_head, precision=highest))
    return (
        jnp.concatenate(query_parts, axis=1),
        jnp.concatenate(key_parts, axis=1),
        jnp.concatenate(value_parts, axis=1),
    )


def widen(source, pieces, reach):
    return jnp.concatenate(pieces[:reach] + [source] + pieces[reach:], axis=3)


def width_slices(source, reach, cols_local):
    margin = reach * cols_local
    slices = []
    for slot in range(2 * reach):
        if slot < reach:
            begin = slot * cols_local
        else:
            begin = margin + cols_local + (slot - reach) * cols_local
        slices.append(source[:, :, :, begin : begin + cols_local])
    return slices


def settle_rows(source, from_below, from_above, rows_local):
    inner = source[:, :, TILE : TILE + rows_local]
    return inner + from_below + from_above


def body(query_field, key_field, value_field, output_grad):
    frames, rows_local, cols_local, channels = query_field.shape
    reach = (max(2 * TILE - cols_local, TILE) + cols_local - 1) // cols_local
    margin = reach * cols_local
    height_index = lax.axis_index("ha")
    width_index = lax.axis_index("wa")
    height_total = rows_local * lax.axis_size("ha")
    width_total = cols_local * lax.axis_size("wa")
    offsets = list(range(reach, 0, -1)) + list(range(-1, -reach - 1, -1))
    stacked = jnp.stack([key_field, value_field])
    anchor = jnp.int32(0)
    first_col = width_index * cols_local
    tile_col = first_col // TILE
    column_start = margin - first_col % TILE - TILE
    pieces = []
    for distance in offsets:
        pieces.append(passed_along(stacked, "wa", distance))
    trimmed = lax.dynamic_slice_in_dim(widen(stacked, pieces, reach), column_start, 3 * TILE, 3)
    extended = extended_2(trimmed, (("ha", 2),), TILE)
    window_span = jnp.arange(3 * TILE, dtype=jnp.int32)
    cols_global = tile_col * TILE - TILE + window_span
    col_ok = (cols_global >= 0) & (cols_global < width_total)
    window_shape = (2, frames, 3 * TILE, 3 * TILE, channels)
    query_rows = query_field.reshape(-1, channels)
    grad_rows = output_grad.reshape(-1, channels)
    key_rows = extended[0].reshape(-1, channels)
    value_rows = extended[1].reshape(-1, channels)
    rows_global = height_index * rows_local + 0 - TILE + window_span
    row_ok = (rows_global >= 0) & (rows_global < height_total)
    plane_ok = row_ok[:, None] & col_ok[None, :]
    key_valid = jnp.broadcast_to(plane_ok[None], (frames, 3 * TILE, 3 * TILE)).reshape(-1)
    query_part, key_part, value_part = tile_grads(
        query_rows, grad_rows, key_rows, value_rows, key_valid
    )
    update = jnp.stack([key_part, value_part]).reshape(window_shape)
    query_blocks = query_part.reshape(frames, TILE, cols_local, channels)
    rims = []
    for rim_part, distance in ((update[:, :, :TILE], -1), (update[:, :, TILE + rows_local :], 1)):
        rims.append(passed_along(rim_part, "ha", distance))
    settled_window = settle_rows(update, rims[0], rims[1], rows_local)
    frame_shape = (2, frames, rows_local, cols_local + 2 * margin, channels)
    settled = lax.dynamic_update_slice(
        jnp.zeros(frame_shape, jnp.float32),
        settled_window,
        (anchor, anchor, anchor, column_start, anchor),
    )
    final = settled[:, :, :, margin : margin + cols_local]
    slices = width_slices(settled, reach, cols_local)
    for slot in range(2 * reach):
        final = final + passed_along(slices[slot], "wa", -offsets[slot])
    return (query_blocks, final[0], final[1])


def solution(mesh):
    placed = (
        P(None, "ha", "wa", None),
        P(None, "ha", "wa", None),
        P(None, "ha", "wa", None),
        P(None, "ha", "wa", None),
    )
    return jax.shard_map(
        body,
        mesh=mesh,
        in_specs=placed,
        out_specs=(P(None, "ha", "wa", None), P(None, "ha", "wa", None), P(None, "ha", "wa", None)),
        check_vma=False,
    )
```

profile of v0, /device:TPU:53, one launch (start us, length us, event | category | flops | bytes accessed | tf_op | source)
XLA Modules:
  0.0 666.2 jit_solution(13458985748511080060)
XLA Ops:
  1.7 8.5 %collective-permute-start = (f32[2,2,16,4,256]{4,3,2,1,0:T(4,128)S(1)}, f32[2,2,16,4,256]{4,3,2,1,0:T(4,128)S(1)}, u32[]{:S(2)}, u32[]{:S(2)}) collective-permute-start(f32[2,2,16,4,256]{4,3,2,1,0:T(4,128)S(1)} %pad_maximum_fusion.4), channel_id=1, source_target_pairs={{0,7},{1,8},{2,9},{3,10},{4,11},{5,12},{6,13},{7,14},{8,15},{9,16}... | collective-permute-start | bytes 786440 | tf_op jit(solution)/shard_map/ppermute | solution.py:14
  10.1 1.9 collective-permute-start.1
  12.1 2.8 collective-permute-start.2
  14.9 2.2 collective-permute-start.3
  17.1 1.9 collective-permute-start.4
  19.0 7.6 %collective-permute-done = f32[2,2,16,4,256]{4,3,2,1,0:T(4,128)S(1)} collective-permute-done((f32[2,2,16,4,256]{4,3,2,1,0:T(4,128)S(1)}, f32[2,2,16,4,256]{4,3,2,1,0:T(4,128)S(1)}, u32[]{:S(2)}, u32[]{:S(2)}) %collective-permute-start) | collective-permute-done | bytes 262176 | tf_op jit(solution)/shard_map/ppermute | solution.py:14
  26.6 5.0 collective-permute-start.5
  31.7 13.2 %collective-permute-done.1 = f32[2,2,16,4,256]{4,3,2,1,0:T(4,128)S(1)} collective-permute-done((f32[2,2,16,4,256]{4,3,2,1,0:T(4,128)S(1)}, f32[2,2,16,4,256]{4,3,2,1,0:T(4,128)S(1)}, u32[]{:S(2)}, u32[]{:S(2)}) %collective-permute-start.1) | collective-permute-done | bytes 262176 | tf_op jit(solution)/shard_map/ppermute | solution.py:14
  44.9 3.2 collective-permute-start.6
  48.1 15.4 %collective-permute-done.2 = f32[2,2,16,4,256]{4,3,2,1,0:T(4,128)S(1)} collective-permute-done((f32[2,2,16,4,256]{4,3,2,1,0:T(4,128)S(1)}, f32[2,2,16,4,256]{4,3,2,1,0:T(4,128)S(1)}, u32[]{:S(2)}, u32[]{:S(2)}) %collective-permute-start.2) | collective-permute-done | bytes 262176 | tf_op jit(solution)/shard_map/ppermute | solution.py:14
  65.4 2.4 collective-permute-done.3
  69.8 9.2 %collective-permute-start.9 = (f32[2,2,16,4,256]{4,3,2,1,0:T(4,128)S(1)}, f32[2,2,16,4,256]{4,3,2,1,0:T(4,128)S(1)}, u32[]{:S(2)}, u32[]{:S(2)}) collective-permute-start(f32[2,2,16,4,256]{4,3,2,1,0:T(4,128)S(1)} %pad_maximum_fusion.4), channel_id=1, source_target_pairs={{3,0},{4,1},{5,2},{6,3},{7,4},{8,5},{9,6},{10,7},{11,8},{12,9},{13... | collective-permute-start | bytes 786440 | tf_op jit(solution)/shard_map/ppermute | solution.py:14
  79.0 5.2 collective-permute-start.10
  84.2 4.4 collective-permute-start.11
  88.7 5.8 collective-permute-start.12
  94.5 1.9 collective-permute-start.13
  96.4 19.8 %collective-permute-done.11 = f32[2,2,16,4,256]{4,3,2,1,0:T(4,128)S(1)} collective-permute-done((f32[2,2,16,4,256]{4,3,2,1,0:T(4,128)S(1)}, f32[2,2,16,4,256]{4,3,2,1,0:T(4,128)S(1)}, u32[]{:S(2)}, u32[]{:S(2)}) %collective-permute-start.11) | collective-permute-done | bytes 262176 | tf_op jit(solution)/shard_map/ppermute | solution.py:14
  116.3 11.0 %collective-permute-done.12 = f32[2,2,16,4,256]{4,3,2,1,0:T(4,128)} collective-permute-done((f32[2,2,16,4,256]{4,3,2,1,0:T(4,128)S(1)}, f32[2,2,16,4,256]{4,3,2,1,0:T(4,128)}, u32[]{:S(2)}, u32[]{:S(2)}) %collective-permute-start.12) | collective-permute-done | bytes 262176 | tf_op jit(solution)/shard_map/ppermute | solution.py:14
  127.2 20.3 %collective-permute-done.13 = f32[2,2,16,4,256]{4,3,2,1,0:T(4,128)} collective-permute-done((f32[2,2,16,4,256]{4,3,2,1,0:T(4,128)S(1)}, f32[2,2,16,4,256]{4,3,2,1,0:T(4,128)}, u32[]{:S(2)}, u32[]{:S(2)}) %collective-permute-start.13) | collective-permute-done | bytes 262176 | tf_op jit(solution)/shard_map/ppermute | solution.py:14
  147.5 9.5 %concatenate.16 = f32[2,2,16,60,256]{4,3,2,1,0:T(8,128)} concatenate(f32[2,2,16,4,256]{4,3,2,1,0:T(4,128)S(1)} %collective-permute-done, f32[2,2,16,4,256]{4,3,2,1,0:T(4,128)S(1)} %collective-permute-done.1, f32[2,2,16,4,256]{4,3,2,1,0:T(4,128)S(1)} %collective-permute-done.2, f32[2,2,16,4,256]{4,3,2,1,0:T(4,128)S(1)} %collective-permute-done.3, ...), dimensions={3} | concatenate | bytes 7864320 | tf_op jit(solution)/shard_map/concatenate | solution.py:63
  156.9 2.6 constant_dynamic-slice_fusion
  159.5 2.7 collective-permute-start.15
  162.3 3.1 collective-permute-start.14
  166.8 64.9 %collective-permute-done.15 = f32[2,2,16,48,256]{4,3,2,1,0:T(8,128)} collective-permute-done((f32[2,2,16,48,256]{4,3,2,1,0:T(8,128)S(1)}, f32[2,2,16,48,256]{4,3,2,1,0:T(8,128)}, u32[]{:S(2)}, u32[]{:S(2)}) %collective-permute-start.15) | collective-permute-done | bytes 3145760 | tf_op jit(solution)/shard_map/ppermute | solution.py:25
  231.7 64.0 %collective-permute-done.14 = f32[2,2,16,48,256]{4,3,2,1,0:T(8,128)} collective-permute-done((f32[2,2,16,48,256]{4,3,2,1,0:T(8,128)S(1)}, f32[2,2,16,48,256]{4,3,2,1,0:T(8,128)}, u32[]{:S(2)}, u32[]{:S(2)}) %collective-permute-start.14) | collective-permute-done | bytes 3145760 | tf_op jit(solution)/shard_map/ppermute | solution.py:24
  295.7 7.4 %pad_maximum_fusion = f32[2,2,48,48,256]{4,3,2,1,0:T(8,128)} fusion(f32[2,2,16,48,256]{4,3,2,1,0:T(8,128)} %collective-permute-done.15, f32[2,2,16,48,256]{4,3,2,1,0:T(8,128)S(1)} %constant_dynamic-slice_fusion, f32[2,2,16,48,256]{4,3,2,1,0:T(8,128)} %collective-permute-done.14), kind=kLoop, calls=%fused_computation.4 | loop fusion | flops 4718592 | bytes 18874368 | tf_op jit(solution)/shard_map/concatenate | solution.py:26
  303.1 4.7 fusion.59
  307.8 2.4 fusion.62
  310.8 4.1 fusion.16
  314.8 2.8 multiply_reduce_fusion
  317.6 2.6 fusion.63
  320.6 2.7 multiply_reduce_fusion.1
  323.4 4.1 fusion.18
  327.4 2.9 fusion.45
  330.4 2.9 fusion.48
  333.3 2.7 pad_maximum_fusion.1
  336.0 6.1 copy.18
  342.1 4.9 pad_maximum_fusion.2
  347.0 6.1 copy.19
  353.1 3.7 fusion
  356.8 3.1 collective-permute-start.17
  359.9 3.4 collective-permute-start.16
  363.3 66.5 %collective-permute-done.17 = f32[2,2,16,48,256]{4,3,2,1,0:T(8,128)S(1)} collective-permute-done((f32[2,2,16,48,256]{4,3,2,1,0:T(8,128)S(1)}, f32[2,2,16,48,256]{4,3,2,1,0:T(8,128)S(1)}, u32[]{:S(2)}, u32[]{:S(2)}) %collective-permute-start.17) | collective-permute-done | bytes 3145760 | tf_op jit(solution)/shard_map/ppermute | solution.py:14
  429.7 65.6 %collective-permute-done.16 = f32[2,2,16,48,256]{4,3,2,1,0:T(8,128)S(1)} collective-permute-done((f32[2,2,16,48,256]{4,3,2,1,0:T(8,128)S(1)}, f32[2,2,16,48,256]{4,3,2,1,0:T(8,128)S(1)}, u32[]{:S(2)}, u32[]{:S(2)}) %collective-permute-start.16) | collective-permute-done | bytes 3145760 | tf_op jit(solution)/shard_map/ppermute | solution.py:14
  495.4 2.6 fusion.3
  498.0 2.5 broadcast_in_dim.15
  500.6 16.2 %dynamic_update_slice.3 = f32[2,2,16,60,256]{4,3,2,1,0:T(8,128)} dynamic-update-slice(f32[2,2,16,60,256]{4,3,2,1,0:T(8,128)} %broadcast_in_dim.15, f32[2,2,16,48,256]{4,3,2,1,0:T(8,128)} %fusion.3, s32[]{:T(128)} %constant.44.clone.1, s32[]{:T(128)} %constant.44.clone.1, s32[]{:T(128)} %constant.44.clone.1, s32[]{:T(128)S(6)} %select_n.28, s32[]{:T(128)} %constant.44.clone.1) | dynamic-update-slice | bytes 6291460 | tf_op jit(solution)/shard_map/dynamic_update_slice | solution.py:124
  516.8 4.8 fusion.60
  521.6 6.1 collective-permute-start.31
  535.4 19.9 %collective-permute-done.31 = f32[2,2,16,4,256]{4,3,2,1,0:T(4,128)S(1)} collective-permute-done((f32[2,2,16,4,256]{4,3,2,1,0:T(4,128)S(1)}, f32[2,2,16,4,256]{4,3,2,1,0:T(4,128)S(1)}, u32[]{:S(2)}, u32[]{:S(2)}) %collective-permute-start.31) | collective-permute-done | bytes 262176 | tf_op jit(solution)/shard_map/ppermute | solution.py:14
  557.3 8.7 %collective-permute-done.30 = f32[2,2,16,4,256]{4,3,2,1,0:T(4,128)S(1)} collective-permute-done((f32[2,2,16,4,256]{4,3,2,1,0:T(4,128)S(1)}, f32[2,2,16,4,256]{4,3,2,1,0:T(4,128)S(1)}, u32[]{:S(2)}, u32[]{:S(2)}) %collective-permute-start.30) | collective-permute-done | bytes 262176 | tf_op jit(solution)/shard_map/ppermute | solution.py:14
  568.0 10.5 %collective-permute-start.24 = (f32[2,2,16,4,256]{4,3,2,1,0:T(4,128)S(1)}, f32[2,2,16,4,256]{4,3,2,1,0:T(4,128)S(1)}, u32[]{:S(2)}, u32[]{:S(2)}) collective-permute-start(f32[2,2,16,4,256]{4,3,2,1,0:T(4,128)S(1)} %get-tuple-element.18), channel_id=1, source_target_pairs={{1,0},{2,1},{3,2},{4,3},{5,4},{6,5},{7,6},{8,7},{9,8},{10,9},{11,1... | collective-permute-start | bytes 786440 | tf_op jit(solution)/shard_map/ppermute | solution.py:14
  578.5 7.0 %collective-permute-start.23 = (f32[2,2,16,4,256]{4,3,2,1,0:T(4,128)S(1)}, f32[2,2,16,4,256]{4,3,2,1,0:T(4,128)S(1)}, u32[]{:S(2)}, u32[]{:S(2)}) collective-permute-start(f32[2,2,16,4,256]{4,3,2,1,0:T(4,128)S(1)} %get-tuple-element.19), channel_id=1, source_target_pairs={{2,0},{3,1},{4,2},{5,3},{6,4},{7,5},{8,6},{9,7},{10,8},{11,9},{12,... | collective-permute-start | bytes 786440 | tf_op jit(solution)/shard_map/ppermute | solution.py:14
  585.5 6.0 fusion.27
  591.6 2.4 collective-permute-start.22
  594.0 2.4 collective-permute-start.21
  596.5 3.2 collective-permute-start.20
  599.7 2.0 collective-permute-start.19
  601.7 5.0 collective-permute-start.18
  606.7 6.0 fusion.24
  613.6 10.5 %collective-permute-done.20 = f32[2,2,16,4,256]{4,3,2,1,0:T(4,128)} collective-permute-done((f32[2,2,16,4,256]{4,3,2,1,0:T(4,128)}, f32[2,2,16,4,256]{4,3,2,1,0:T(4,128)}, u32[]{:S(2)}, u32[]{:S(2)}) %collective-permute-start.20) | collective-permute-done | bytes 262176 | tf_op jit(solution)/shard_map/ppermute | solution.py:14
  624.1 21.5 %collective-permute-done.19 = f32[2,2,16,4,256]{4,3,2,1,0:T(4,128)} collective-permute-done((f32[2,2,16,4,256]{4,3,2,1,0:T(4,128)S(1)}, f32[2,2,16,4,256]{4,3,2,1,0:T(4,128)}, u32[]{:S(2)}, u32[]{:S(2)}) %collective-permute-start.19) | collective-permute-done | bytes 262176 | tf_op jit(solution)/shard_map/ppermute | solution.py:14
  645.7 17.1 %collective-permute-done.18 = f32[2,2,16,4,256]{4,3,2,1,0:T(4,128)} collective-permute-done((f32[2,2,16,4,256]{4,3,2,1,0:T(4,128)S(1)}, f32[2,2,16,4,256]{4,3,2,1,0:T(4,128)}, u32[]{:S(2)}, u32[]{:S(2)}) %collective-permute-start.18) | collective-permute-done | bytes 262176 | tf_op jit(solution)/shard_map/ppermute | solution.py:14
  662.7 2.5 add_add_fusion
  (82 shorter events, 20.3 us)
Async XLA Ops:
  1.7 25.0 %collective-permute-start = (f32[2,2,16,4,256]{4,3,2,1,0:T(4,128)S(1)}, f32[2,2,16,4,256]{4,3,2,1,0:T(4,128)S(1)}, u32[]{:S(2)}, u32[]{:S(2)}) collective-permute-start(f32[2,2,16,4,256]{4,3,2,1,0:T(4,128)S(1)} %pad_maximum_fusion.4), channel_id=1, source_target_pairs={{0,7},{1,8},{2,9},{3,10},{4,11},{5,12},{6,13},{7,14},{8,15},{9,16}... | collective-permute-start | bytes 786440 | tf_op jit(solution)/shard_map/ppermute | solution.py:14
  10.1 34.7 %collective-permute-start.1 = (f32[2,2,16,4,256]{4,3,2,1,0:T(4,128)S(1)}, f32[2,2,16,4,256]{4,3,2,1,0:T(4,128)S(1)}, u32[]{:S(2)}, u32[]{:S(2)}) collective-permute-start(f32[2,2,16,4,256]{4,3,2,1,0:T(4,128)S(1)} %pad_maximum_fusion.4), channel_id=1, source_target_pairs={{0,6},{1,7},{2,8},{3,9},{4,10},{5,11},{6,12},{7,13},{8,14},{9,15},... | collective-permute-start | bytes 786440 | tf_op jit(solution)/shard_map/ppermute | solution.py:14
  12.1 51.4 %collective-permute-start.2 = (f32[2,2,16,4,256]{4,3,2,1,0:T(4,128)S(1)}, f32[2,2,16,4,256]{4,3,2,1,0:T(4,128)S(1)}, u32[]{:S(2)}, u32[]{:S(2)}) collective-permute-start(f32[2,2,16,4,256]{4,3,2,1,0:T(4,128)S(1)} %pad_maximum_fusion.4), channel_id=1, source_target_pairs={{0,5},{1,6},{2,7},{3,8},{4,9},{5,10},{6,11},{7,12},{8,13},{9,14},{... | collective-permute-start | bytes 786440 | tf_op jit(solution)/shard_map/ppermute | solution.py:14
  14.9 52.9 %collective-permute-start.3 = (f32[2,2,16,4,256]{4,3,2,1,0:T(4,128)S(1)}, f32[2,2,16,4,256]{4,3,2,1,0:T(4,128)S(1)}, u32[]{:S(2)}, u32[]{:S(2)}) collective-permute-start(f32[2,2,16,4,256]{4,3,2,1,0:T(4,128)S(1)} %pad_maximum_fusion.4), channel_id=1, source_target_pairs={{0,4},{1,5},{2,6},{3,7},{4,8},{5,9},{6,10},{7,11},{8,12},{9,13},{1... | collective-permute-start | bytes 786440 | tf_op jit(solution)/shard_map/ppermute | solution.py:14
  17.1 52.7 %collective-permute-start.4 = (f32[2,2,16,4,256]{4,3,2,1,0:T(4,128)S(1)}, f32[2,2,16,4,256]{4,3,2,1,0:T(4,128)S(1)}, u32[]{:S(2)}, u32[]{:S(2)}) collective-permute-start(f32[2,2,16,4,256]{4,3,2,1,0:T(4,128)S(1)} %pad_maximum_fusion.4), channel_id=1, source_target_pairs={{0,3},{1,4},{2,5},{3,6},{4,7},{5,8},{6,9},{7,10},{8,11},{9,12},{10... | collective-permute-start | bytes 786440 | tf_op jit(solution)/shard_map/ppermute | solution.py:14
  26.6 52.3 %collective-permute-start.5 = (f32[2,2,16,4,256]{4,3,2,1,0:T(4,128)S(1)}, f32[2,2,16,4,256]{4,3,2,1,0:T(4,128)S(1)}, u32[]{:S(2)}, u32[]{:S(2)}) collective-permute-start(f32[2,2,16,4,256]{4,3,2,1,0:T(4,128)S(1)} %pad_maximum_fusion.4), channel_id=1, source_target_pairs={{0,2},{1,3},{2,4},{3,5},{4,6},{5,7},{6,8},{7,9},{8,10},{9,11},{10,... | collective-permute-start | bytes 786440 | tf_op jit(solution)/shard_map/ppermute | solution.py:14
  44.9 39.3 %collective-permute-start.6 = (f32[2,2,16,4,256]{4,3,2,1,0:T(4,128)S(1)}, f32[2,2,16,4,256]{4,3,2,1,0:T(4,128)S(1)}, u32[]{:S(2)}, u32[]{:S(2)}) collective-permute-start(f32[2,2,16,4,256]{4,3,2,1,0:T(4,128)S(1)} %pad_maximum_fusion.4), channel_id=1, source_target_pairs={{0,1},{1,2},{2,3},{3,4},{4,5},{5,6},{6,7},{7,8},{8,9},{9,10},{10,1... | collective-permute-start | bytes 786440 | tf_op jit(solution)/shard_map/ppermute | solution.py:14
  63.5 25.2 %collective-permute-start.7 = (f32[2,2,16,4,256]{4,3,2,1,0:T(4,128)S(1)}, f32[2,2,16,4,256]{4,3,2,1,0:T(4,128)S(1)}, u32[]{:S(2)}, u32[]{:S(2)}) collective-permute-start(f32[2,2,16,4,256]{4,3,2,1,0:T(4,128)S(1)} %pad_maximum_fusion.4), channel_id=1, source_target_pairs={{1,0},{2,1},{3,2},{4,3},{5,4},{6,5},{7,6},{8,7},{9,8},{10,9},{11,1... | collective-permute-start | bytes 786440 | tf_op jit(solution)/shard_map/ppermute | solution.py:14
  67.8 26.6 %collective-permute-start.8 = (f32[2,2,16,4,256]{4,3,2,1,0:T(4,128)S(1)}, f32[2,2,16,4,256]{4,3,2,1,0:T(4,128)S(1)}, u32[]{:S(2)}, u32[]{:S(2)}) collective-permute-start(f32[2,2,16,4,256]{4,3,2,1,0:T(4,128)S(1)} %pad_maximum_fusion.4), channel_id=1, source_target_pairs={{2,0},{3,1},{4,2},{5,3},{6,4},{7,5},{8,6},{9,7},{10,8},{11,9},{12,... | collective-permute-start | bytes 786440 | tf_op jit(solution)/shard_map/ppermute | solution.py:14
  69.8 26.6 %collective-permute-start.9 = (f32[2,2,16,4,256]{4,3,2,1,0:T(4,128)S(1)}, f32[2,2,16,4,256]{4,3,2,1,0:T(4,128)S(1)}, u32[]{:S(2)}, u32[]{:S(2)}) collective-permute-start(f32[2,2,16,4,256]{4,3,2,1,0:T(4,128)S(1)} %pad_maximum_fusion.4), channel_id=1, source_target_pairs={{3,0},{4,1},{5,2},{6,3},{7,4},{8,5},{9,6},{10,7},{11,8},{12,9},{13... | collective-permute-start | bytes 786440 | tf_op jit(solution)/shard_map/ppermute | solution.py:14
  79.0 17.4 %collective-permute-start.10 = (f32[2,2,16,4,256]{4,3,2,1,0:T(4,128)S(1)}, f32[2,2,16,4,256]{4,3,2,1,0:T(4,128)S(1)}, u32[]{:S(2)}, u32[]{:S(2)}) collective-permute-start(f32[2,2,16,4,256]{4,3,2,1,0:T(4,128)S(1)} %pad_maximum_fusion.4), channel_id=1, source_target_pairs={{4,0},{5,1},{6,2},{7,3},{8,4},{9,5},{10,6},{11,7},{12,8},{13,9},{1... | collective-permute-start | bytes 786440 | tf_op jit(solution)/shard_map/ppermute | solution.py:14
  84.2 32.0 %collective-permute-start.11 = (f32[2,2,16,4,256]{4,3,2,1,0:T(4,128)S(1)}, f32[2,2,16,4,256]{4,3,2,1,0:T(4,128)S(1)}, u32[]{:S(2)}, u32[]{:S(2)}) collective-permute-start(f32[2,2,16,4,256]{4,3,2,1,0:T(4,128)S(1)} %pad_maximum_fusion.4), channel_id=1, source_target_pairs={{5,0},{6,1},{7,2},{8,3},{9,4},{10,5},{11,6},{12,7},{13,8},{14,9},{... | collective-permute-start | bytes 786440 | tf_op jit(solution)/shard_map/ppermute | solution.py:14
  88.7 38.6 %collective-permute-start.12 = (f32[2,2,16,4,256]{4,3,2,1,0:T(4,128)S(1)}, f32[2,2,16,4,256]{4,3,2,1,0:T(4,128)}, u32[]{:S(2)}, u32[]{:S(2)}) collective-permute-start(f32[2,2,16,4,256]{4,3,2,1,0:T(4,128)S(1)} %pad_maximum_fusion.4), channel_id=1, source_target_pairs={{6,0},{7,1},{8,2},{9,3},{10,4},{11,5},{12,6},{13,7},{14,8},{15,9},... | collective-permute-start | bytes 786440 | tf_op jit(solution)/shard_map/ppermute | solution.py:14
  94.5 53.0 %collective-permute-start.13 = (f32[2,2,16,4,256]{4,3,2,1,0:T(4,128)S(1)}, f32[2,2,16,4,256]{4,3,2,1,0:T(4,128)}, u32[]{:S(2)}, u32[]{:S(2)}) collective-permute-start(f32[2,2,16,4,256]{4,3,2,1,0:T(4,128)S(1)} %pad_maximum_fusion.4), channel_id=1, source_target_pairs={{7,0},{8,1},{9,2},{10,3},{11,4},{12,5},{13,6},{14,7},{15,8},{16,9}... | collective-permute-start | bytes 786440 | tf_op jit(solution)/shard_map/ppermute | solution.py:14
  156.9 8.6 %copy-start.14 = (f32[2,16,4,256]{3,2,1,0:T(4,128)S(1)}, f32[2,16,4,256]{3,2,1,0:T(4,128)}, u32[]{:S(2)}) copy-start(f32[2,16,4,256]{3,2,1,0:T(4,128)} %param.4) | copy-start | bytes 393220
  159.5 72.2 %collective-permute-start.15 = (f32[2,2,16,48,256]{4,3,2,1,0:T(8,128)S(1)}, f32[2,2,16,48,256]{4,3,2,1,0:T(8,128)}, u32[]{:S(2)}, u32[]{:S(2)}) collective-permute-start(f32[2,2,16,48,256]{4,3,2,1,0:T(8,128)S(1)} %constant_dynamic-slice_fusion), channel_id=1, source_target_pairs={{32,0},{64,32},{96,64},{128,96},{160,128},{192,160},{224,192},{33,... | collective-permute-start | bytes 9437192 | tf_op jit(solution)/shard_map/ppermute | solution.py:25
  162.3 133.5 %collective-permute-start.14 = (f32[2,2,16,48,256]{4,3,2,1,0:T(8,128)S(1)}, f32[2,2,16,48,256]{4,3,2,1,0:T(8,128)}, u32[]{:S(2)}, u32[]{:S(2)}) collective-permute-start(f32[2,2,16,48,256]{4,3,2,1,0:T(8,128)S(1)} %constant_dynamic-slice_fusion), channel_id=1, source_target_pairs={{0,32},{32,64},{64,96},{96,128},{128,160},{160,192},{192,224},{1,3... | collective-permute-start | bytes 9437192 | tf_op jit(solution)/shard_map/ppermute | solution.py:24
  307.8 9.8 %copy-start.2 = (f32[1,2,48,48,256]{4,3,2,1,0:T(8,128)}, f32[1,2,48,48,256]{4,3,2,1,0:T(8,128)S(1)}, u32[]{:S(2)}) copy-start(f32[1,2,48,48,256]{4,3,2,1,0:T(8,128)S(1)} %get-tuple-element.9) | copy-start | bytes 14155780
  310.3 17.2 %copy-start = (f32[128,4608]{1,0:T(8,128)}, f32[128,4608]{1,0:T(8,128)S(1)}, u32[]{:S(2)}) copy-start(f32[128,4608]{1,0:T(8,128)S(1)} %get-tuple-element.29) | copy-start | bytes 7077892
  317.6 9.9 %copy-start.5 = (f32[128,4608]{1,0:T(8,128)}, f32[128,4608]{1,0:T(8,128)S(1)}, u32[]{:S(2)}) copy-start(f32[128,4608]{1,0:T(8,128)S(1)} %get-tuple-element.31) | copy-start | bytes 7077892
  323.4 7.0 %copy-start.3 = (f32[128,4608]{1,0:T(8,128)}, f32[128,4608]{1,0:T(8,128)S(1)}, u32[]{:S(2)}) copy-start(f32[128,4608]{1,0:T(8,128)S(1)} %get-tuple-element.35) | copy-start | bytes 7077892
  353.1 142.2 %slice-start = ((s8[4718592]{0:T(1024)(128)(4,1)}), s8[4194304]{0:T(1024)(128)(4,1)S(1)}, s32[]{:S(2)}) async-start(s8[4718592]{0:T(1024)(128)(4,1)} %bitcast.19), calls=%async_computation | async-start | bytes 8388608
  353.1 142.2 %slice-start.2 = ((s8[4718592]{0:T(1024)(128)(4,1)}), s8[4194304]{0:T(1024)(128)(4,1)S(1)}, s32[]{:S(2)}) async-start(s8[4718592]{0:T(1024)(128)(4,1)} %bitcast.23), calls=%async_computation.2 | async-start | bytes 8388608
  353.1 142.2 %slice-start.1 = ((s8[4718592]{0:T(1024)(128)(4,1)}), s8[524288]{0:T(1024)(128)(4,1)S(1)}, s32[]{:S(2)}) async-start(s8[4718592]{0:T(1024)(128)(4,1)} %bitcast.19), calls=%async_computation.1 | async-start | bytes 1048576
  353.1 142.2 %slice-start.3 = ((s8[4718592]{0:T(1024)(128)(4,1)}), s8[524288]{0:T(1024)(128)(4,1)S(1)}, s32[]{:S(2)}) async-start(s8[4718592]{0:T(1024)(128)(4,1)} %bitcast.23), calls=%async_computation.3 | async-start | bytes 1048576
  356.8 72.9 %collective-permute-start.17 = (f32[2,2,16,48,256]{4,3,2,1,0:T(8,128)S(1)}, f32[2,2,16,48,256]{4,3,2,1,0:T(8,128)S(1)}, u32[]{:S(2)}, u32[]{:S(2)}) collective-permute-start(f32[2,2,16,48,256]{4,3,2,1,0:T(8,128)S(1)} %get-tuple-element.7), channel_id=1, source_target_pairs={{0,32},{32,64},{64,96},{96,128},{128,160},{160,192},{192,224},{1,3... | collective-permute-start | bytes 9437192 | tf_op jit(solution)/shard_map/ppermute | solution.py:14
  359.9 135.5 %collective-permute-start.16 = (f32[2,2,16,48,256]{4,3,2,1,0:T(8,128)S(1)}, f32[2,2,16,48,256]{4,3,2,1,0:T(8,128)S(1)}, u32[]{:S(2)}, u32[]{:S(2)}) collective-permute-start(f32[2,2,16,48,256]{4,3,2,1,0:T(8,128)S(1)} %get-tuple-element.6), channel_id=1, source_target_pairs={{32,0},{64,32},{96,64},{128,96},{160,128},{192,160},{224,192},{33,... | collective-permute-start | bytes 9437192 | tf_op jit(solution)/shard_map/ppermute | solution.py:14
  516.8 68.8 %copy-start.1 = (f32[128,4608]{1,0:T(8,128)S(1)}, f32[128,4608]{1,0:T(8,128)}, u32[]{:S(2)}) copy-start(f32[128,4608]{1,0:T(8,128)} %copy-done) | copy-start | bytes 7077892
  516.8 68.8 %copy-start.6 = (f32[128,4608]{1,0:T(8,128)S(1)}, f32[128,4608]{1,0:T(8,128)}, u32[]{:S(2)}) copy-start(f32[128,4608]{1,0:T(8,128)} %copy-done.5) | copy-start | bytes 7077892
  521.6 33.8 %collective-permute-start.31 = (f32[2,2,16,4,256]{4,3,2,1,0:T(4,128)S(1)}, f32[2,2,16,4,256]{4,3,2,1,0:T(4,128)S(1)}, u32[]{:S(2)}, u32[]{:S(2)}) collective-permute-start(f32[2,2,16,4,256]{4,3,2,1,0:T(4,128)S(1)} %get-tuple-element.11), channel_id=1, source_target_pairs={{0,7},{1,8},{2,9},{3,10},{4,11},{5,12},{6,13},{7,14},{8,15},{9,16}... | collective-permute-start | bytes 786440 | tf_op jit(solution)/shard_map/ppermute | solution.py:14
  527.7 38.3 %collective-permute-start.30 = (f32[2,2,16,4,256]{4,3,2,1,0:T(4,128)S(1)}, f32[2,2,16,4,256]{4,3,2,1,0:T(4,128)S(1)}, u32[]{:S(2)}, u32[]{:S(2)}) collective-permute-start(f32[2,2,16,4,256]{4,3,2,1,0:T(4,128)S(1)} %get-tuple-element.12), channel_id=1, source_target_pairs={{0,6},{1,7},{2,8},{3,9},{4,10},{5,11},{6,12},{7,13},{8,14},{9,15},... | collective-permute-start | bytes 786440 | tf_op jit(solution)/shard_map/ppermute | solution.py:14
  529.7 38.3 %collective-permute-start.29 = (f32[2,2,16,4,256]{4,3,2,1,0:T(4,128)S(1)}, f32[2,2,16,4,256]{4,3,2,1,0:T(4,128)S(1)}, u32[]{:S(2)}, u32[]{:S(2)}) collective-permute-start(f32[2,2,16,4,256]{4,3,2,1,0:T(4,128)S(1)} %get-tuple-element.13), channel_id=1, source_target_pairs={{0,5},{1,6},{2,7},{3,8},{4,9},{5,10},{6,11},{7,12},{8,13},{9,14},{... | collective-permute-start | bytes 786440 | tf_op jit(solution)/shard_map/ppermute | solution.py:14
  531.6 46.9 %collective-permute-start.28 = (f32[2,2,16,4,256]{4,3,2,1,0:T(4,128)S(1)}, f32[2,2,16,4,256]{4,3,2,1,0:T(4,128)S(1)}, u32[]{:S(2)}, u32[]{:S(2)}) collective-permute-start(f32[2,2,16,4,256]{4,3,2,1,0:T(4,128)S(1)} %get-tuple-element.14), channel_id=1, source_target_pairs={{0,4},{1,5},{2,6},{3,7},{4,8},{5,9},{6,10},{7,11},{8,12},{9,13},{1... | collective-permute-start | bytes 786440 | tf_op jit(solution)/shard_map/ppermute | solution.py:14
  533.5 58.1 %collective-permute-start.27 = (f32[2,2,16,4,256]{4,3,2,1,0:T(4,128)S(1)}, f32[2,2,16,4,256]{4,3,2,1,0:T(4,128)S(1)}, u32[]{:S(2)}, u32[]{:S(2)}) collective-permute-start(f32[2,2,16,4,256]{4,3,2,1,0:T(4,128)S(1)} %get-tuple-element.15), channel_id=1, source_target_pairs={{0,3},{1,4},{2,5},{3,6},{4,7},{5,8},{6,9},{7,10},{8,11},{9,12},{10... | collective-permute-start | bytes 786440 | tf_op jit(solution)/shard_map/ppermute | solution.py:14
  555.4 38.6 %collective-permute-start.26 = (f32[2,2,16,4,256]{4,3,2,1,0:T(4,128)S(1)}, f32[2,2,16,4,256]{4,3,2,1,0:T(4,128)S(1)}, u32[]{:S(2)}, u32[]{:S(2)}) collective-permute-start(f32[2,2,16,4,256]{4,3,2,1,0:T(4,128)S(1)} %get-tuple-element.16), channel_id=1, source_target_pairs={{0,2},{1,3},{2,4},{3,5},{4,6},{5,7},{6,8},{7,9},{8,10},{9,11},{10,... | collective-permute-start | bytes 786440 | tf_op jit(solution)/shard_map/ppermute | solution.py:14
  566.0 30.5 %collective-permute-start.25 = (f32[2,2,16,4,256]{4,3,2,1,0:T(4,128)S(1)}, f32[2,2,16,4,256]{4,3,2,1,0:T(4,128)S(1)}, u32[]{:S(2)}, u32[]{:S(2)}) collective-permute-start(f32[2,2,16,4,256]{4,3,2,1,0:T(4,128)S(1)} %get-tuple-element.17), channel_id=1, source_target_pairs={{0,1},{1,2},{2,3},{3,4},{4,5},{5,6},{6,7},{7,8},{8,9},{9,10},{10,1... | collective-permute-start | bytes 786440 | tf_op jit(solution)/shard_map/ppermute | solution.py:14
  567.9 23.6 %copy-start.7 = (f32[2,2,16,4,256]{4,3,2,1,0:T(4,128)}, f32[2,2,16,4,256]{4,3,2,1,0:T(4,128)S(1)}, u32[]{:S(2)}) copy-start(f32[2,2,16,4,256]{4,3,2,1,0:T(4,128)S(1)} %collective-permute-done.29) | copy-start | bytes 786436
  568.0 31.7 %collective-permute-start.24 = (f32[2,2,16,4,256]{4,3,2,1,0:T(4,128)S(1)}, f32[2,2,16,4,256]{4,3,2,1,0:T(4,128)S(1)}, u32[]{:S(2)}, u32[]{:S(2)}) collective-permute-start(f32[2,2,16,4,256]{4,3,2,1,0:T(4,128)S(1)} %get-tuple-element.18), channel_id=1, source_target_pairs={{1,0},{2,1},{3,2},{4,3},{5,4},{6,5},{7,6},{8,7},{9,8},{10,9},{11,1... | collective-permute-start | bytes 786440 | tf_op jit(solution)/shard_map/ppermute | solution.py:14
  578.5 13.1 %copy-start.8 = (f32[2,2,16,4,256]{4,3,2,1,0:T(4,128)}, f32[2,2,16,4,256]{4,3,2,1,0:T(4,128)S(1)}, u32[]{:S(2)}) copy-start(f32[2,2,16,4,256]{4,3,2,1,0:T(4,128)S(1)} %collective-permute-done.28) | copy-start | bytes 786436
  578.5 28.2 %copy-start.4 = (f32[128,4608]{1,0:T(8,128)S(1)}, f32[128,4608]{1,0:T(8,128)}, u32[]{:S(2)}) copy-start(f32[128,4608]{1,0:T(8,128)} %copy-done.3) | copy-start | bytes 7077892
  578.5 23.1 %collective-permute-start.23 = (f32[2,2,16,4,256]{4,3,2,1,0:T(4,128)S(1)}, f32[2,2,16,4,256]{4,3,2,1,0:T(4,128)S(1)}, u32[]{:S(2)}, u32[]{:S(2)}) collective-permute-start(f32[2,2,16,4,256]{4,3,2,1,0:T(4,128)S(1)} %get-tuple-element.19), channel_id=1, source_target_pairs={{2,0},{3,1},{4,2},{5,3},{6,4},{7,5},{8,6},{9,7},{10,8},{11,9},{12,... | collective-permute-start | bytes 786440 | tf_op jit(solution)/shard_map/ppermute | solution.py:14
  591.6 10.1 %copy-start.9 = (f32[2,2,16,4,256]{4,3,2,1,0:T(4,128)}, f32[2,2,16,4,256]{4,3,2,1,0:T(4,128)S(1)}, u32[]{:S(2)}) copy-start(f32[2,2,16,4,256]{4,3,2,1,0:T(4,128)S(1)} %collective-permute-done.27) | copy-start | bytes 786436
  591.6 22.0 %collective-permute-start.22 = (f32[2,2,16,4,256]{4,3,2,1,0:T(4,128)}, f32[2,2,16,4,256]{4,3,2,1,0:T(4,128)}, u32[]{:S(2)}, u32[]{:S(2)}) collective-permute-start(f32[2,2,16,4,256]{4,3,2,1,0:T(4,128)} %get-tuple-element.20), channel_id=1, source_target_pairs={{3,0},{4,1},{5,2},{6,3},{7,4},{8,5},{9,6},{10,7},{11,8},{12,9},{13... | collective-permute-start | bytes 786440 | tf_op jit(solution)/shard_map/ppermute | solution.py:14
  594.0 18.7 %copy-start.10 = (f32[2,2,16,4,256]{4,3,2,1,0:T(4,128)}, f32[2,2,16,4,256]{4,3,2,1,0:T(4,128)S(1)}, u32[]{:S(2)}) copy-start(f32[2,2,16,4,256]{4,3,2,1,0:T(4,128)S(1)} %collective-permute-done.26) | copy-start | bytes 786436
  594.0 19.5 %collective-permute-start.21 = (f32[2,2,16,4,256]{4,3,2,1,0:T(4,128)}, f32[2,2,16,4,256]{4,3,2,1,0:T(4,128)}, u32[]{:S(2)}, u32[]{:S(2)}) collective-permute-start(f32[2,2,16,4,256]{4,3,2,1,0:T(4,128)} %get-tuple-element.21), channel_id=1, source_target_pairs={{4,0},{5,1},{6,2},{7,3},{8,4},{9,5},{10,6},{11,7},{12,8},{13,9},{1... | collective-permute-start | bytes 786440 | tf_op jit(solution)/shard_map/ppermute | solution.py:14
  596.5 16.2 %copy-start.11 = (f32[2,2,16,4,256]{4,3,2,1,0:T(4,128)}, f32[2,2,16,4,256]{4,3,2,1,0:T(4,128)S(1)}, u32[]{:S(2)}) copy-start(f32[2,2,16,4,256]{4,3,2,1,0:T(4,128)S(1)} %collective-permute-done.25) | copy-start | bytes 786436
  596.5 27.6 %collective-permute-start.20 = (f32[2,2,16,4,256]{4,3,2,1,0:T(4,128)}, f32[2,2,16,4,256]{4,3,2,1,0:T(4,128)}, u32[]{:S(2)}, u32[]{:S(2)}) collective-permute-start(f32[2,2,16,4,256]{4,3,2,1,0:T(4,128)} %get-tuple-element.22), channel_id=1, source_target_pairs={{5,0},{6,1},{7,2},{8,3},{9,4},{10,5},{11,6},{12,7},{13,8},{14,9},{... | collective-permute-start | bytes 786440 | tf_op jit(solution)/shard_map/ppermute | solution.py:14
  599.7 13.1 %copy-start.12 = (f32[2,2,16,4,256]{4,3,2,1,0:T(4,128)}, f32[2,2,16,4,256]{4,3,2,1,0:T(4,128)S(1)}, u32[]{:S(2)}) copy-start(f32[2,2,16,4,256]{4,3,2,1,0:T(4,128)S(1)} %collective-permute-done.24) | copy-start | bytes 786436
  599.7 46.0 %collective-permute-start.19 = (f32[2,2,16,4,256]{4,3,2,1,0:T(4,128)S(1)}, f32[2,2,16,4,256]{4,3,2,1,0:T(4,128)}, u32[]{:S(2)}, u32[]{:S(2)}) collective-permute-start(f32[2,2,16,4,256]{4,3,2,1,0:T(4,128)S(1)} %get-tuple-element.23), channel_id=1, source_target_pairs={{6,0},{7,1},{8,2},{9,3},{10,4},{11,5},{12,6},{13,7},{14,8},{15,9},... | collective-permute-start | bytes 786440 | tf_op jit(solution)/shard_map/ppermute | solution.py:14
  601.7 11.1 %copy-start.13 = (f32[2,2,16,4,256]{4,3,2,1,0:T(4,128)}, f32[2,2,16,4,256]{4,3,2,1,0:T(4,128)S(1)}, u32[]{:S(2)}) copy-start(f32[2,2,16,4,256]{4,3,2,1,0:T(4,128)S(1)} %collective-permute-done.23) | copy-start | bytes 786436
  601.7 61.1 %collective-permute-start.18 = (f32[2,2,16,4,256]{4,3,2,1,0:T(4,128)S(1)}, f32[2,2,16,4,256]{4,3,2,1,0:T(4,128)}, u32[]{:S(2)}, u32[]{:S(2)}) collective-permute-start(f32[2,2,16,4,256]{4,3,2,1,0:T(4,128)S(1)} %get-tuple-element.10), channel_id=1, source_target_pairs={{7,0},{8,1},{9,2},{10,3},{11,4},{12,5},{13,6},{14,7},{15,8},{16,9}... | collective-permute-start | bytes 786440 | tf_op jit(solution)/shard_map/ppermute | solution.py:14
where the time goes:
time: 671 us; the launch traced here: 666 us
  waiting for transfers between devices  429 us (64%)
  starting transfers between devices  118 us (18%)
  local copies, waits for them, and re-layouts  55.3 us (8%)
  matrix products  36.4 us (5%)
  other arithmetic  25.9 us (4%)
    ppermute x30, waiting for transfers between devices, passed_along(): return lax.ppermute(block, axis, route)  300 us
    ppermute x30, starting transfers between devices, passed_along(): return lax.ppermute(block, axis, route)  112 us
    ppermute x1, waiting for transfers between devices, extended_2(): after = lax.ppermute(first, axis, down)  64.9 us
    ppermute x1, waiting for transfers between devices, extended_2(): before = lax.ppermute(last, axis, up)  64 us
    dynamic_update_slice x1, local copies, waits for them, and re-layouts, body(): lax.dynamic_update_slice(jnp.zeros(frame_shape, jnp.float32), settled_win...  16.2 us
  transfers between devices with their start and end apart: 32, of which 16 were waited for; matrix products, arithmetic and copies ran while one was open for 2% of the time, Pallas kernels for 0%

commit v1 on v0

v1 whole, which is shorter than its diff:
```python
import jax
import jax.numpy as jnp
from jax import lax
from jax.experimental import pallas as pl
from jax.experimental.pallas import tpu as pltpu
from jax.sharding import PartitionSpec as P

MESH = pl.DeviceIdType.MESH
F32 = jnp.float32
BF16 = jnp.bfloat16
DIM = 128
SCALE = DIM ** -0.5
LOW = -1e30
CELLS = 128
UNIT = 2 * CELLS
HALF = 2 * UNIT


def halves(x):
    hi = x.astype(BF16)
    return hi, (x - hi.astype(F32)).astype(BF16)


def thirds(x):
    hi = x.astype(BF16)
    rest = x - hi.astype(F32)
    mid = rest.astype(BF16)
    return hi, mid, (rest - mid.astype(F32)).astype(BF16)


def dot(a, b, dims):
    return lax.dot_general(a, b, (dims, ((), ())), preferred_element_type=F32)


def kernel(
    x_ref, out_ref,
    sib, kvb, qb, kp, rq, ro, wbuf, dbuf, st, sall, gst, dqt, dqr, own, halo, yret, zret, fin, fout,
    core_sem, near_sem, far_sem, y_sem, zq_sem, xq_sem, stat_sem, yr_sem, zr_sem, dq_sem, fin_sem,
):
    ha, wa = lax.axis_index("ha"), lax.axis_index("wa")
    row, xl = ha // 2, ha % 2
    core = wa % 2
    chip = wa // 2
    zp = chip % 2
    tile = chip // 2
    side = 2 * zp - 1
    up = 2 * xl - 1

    sib_id = (ha, wa + 1 - 2 * core)
    near_id = (ha, (wa + 2 * side + 32) % 32)
    far_to = (ha, (wa - 4 * side + 32) % 32)
    far_from = (ha, (wa + 4 * side + 32) % 32)
    zpair = (ha, wa - 2 * side)
    xpair = (ha - up, wa)
    diag = (ha - up, wa - 2 * side)
    y_to = ((ha + 2 * up + 8) % 8, wa)
    y_from = ((ha - 2 * up + 8) % 8, wa)

    side_in = jnp.where(zp == 0, tile > 0, tile < 7)
    far_out = jnp.where(zp == 0, tile < 7, tile > 0)
    y_out = jnp.where(xl == 1, row < 3, row > 0)
    y_in = jnp.where(xl == 1, row > 0, row < 3)

    def remote(src, dst, sems, index, device):
        return pltpu.make_async_remote_copy(
            src_ref=src, dst_ref=dst, send_sem=sems.at[(0,) + index], recv_sem=sems.at[(1,) + index],
            device_id=device, device_id_type=MESH,
        )

    barrier = pltpu.get_barrier_semaphore()
    partners = (sib_id, near_id, far_to, far_from, zpair, xpair, diag, y_to, y_from)
    for device in partners:
        pl.semaphore_signal(barrier, inc=1, device_id=device, device_id_type=MESH)
    pl.semaphore_wait(barrier, len(partners))

    def core_copy():
        return remote(x_ref.at[1 - core], sib, core_sem, (0,), sib_id)

    def near_copy(src, blk):
        return remote(src, kvb.at[0, 1, blk], near_sem, (blk,), near_id)

    def far_copy(src, blk):
        return remote(src, kvb.at[0, 2, blk], far_sem, (blk,), far_to)

    def y_copy(src, unit, blk):
        return remote(src, kvb.at[1, unit, blk], y_sem, (unit, blk), y_to)

    def zq_copy(src, blk):
        return remote(src, qb.at[xl, zp, blk], zq_sem, (blk,), zpair)

    def xq_copy(src, which, blk):
        place = zp + which - 2 * zp * which
        return remote(src, qb.at[xl, place, blk], xq_sem, (which, blk), xpair)

    def first_sends(kv, q, blk):
        @pl.when(y_out)
        def _():
            y_copy(kv, 0, blk).start()

        @pl.when(side_in)
        def _():
            near_copy(kv, blk).start()

        @pl.when(far_out)
        def _():
            far_copy(kv, blk).start()

        zq_copy(q, blk).start()
        xq_copy(q, 0, blk).start()

    core_copy().start()
    first_sends(x_ref.at[core, pl.ds(0, 2)], x_ref.at[core, pl.ds(2, 2)], core)
    kvb[0, 0, core] = x_ref[core, 0:2]
    qb[xl, zp, core] = x_ref[core, 2:4]
    core_copy().wait_recv()
    first_sends(sib.at[pl.ds(0, 2)], sib.at[pl.ds(2, 2)], 1 - core)
    kvb[0, 0, 1 - core] = sib[0:2]
    qb[xl, zp, 1 - core] = sib[2:4]

    def prepare_queries(half, place):
        for blk in range(2):
            q1, q2, q3 = thirds(qb[half, place, blk, 0] * SCALE)
            o1, o2 = halves(qb[half, place, blk, 1])
            rows = pl.ds(pl.multiple_of(place * UNIT + blk * CELLS, CELLS), CELLS)
            for i, part in enumerate((q1, q1, q2, q2, q3, q1)):
                rq[half, rows, i * DIM:(i + 1) * DIM] = part
            for i, part in enumerate((o1, o1, o2, o2)):
                ro[half, rows, i * DIM:(i + 1) * DIM] = part

    prepare_queries(xl, zp)
    dqt[...] = jnp.zeros_like(dqt)

    for step in range(2):
        blk = core + step - 2 * core * step

        @pl.when(side_in)
        def _():
            near_copy(kvb.at[0, 1, blk], blk).wait_recv()

            @pl.when(y_out)
            def _():
                y_copy(kvb.at[0, 1, blk], 1, blk).start()

            far_copy(kvb.at[0, 2, blk], blk).wait_recv()

            @pl.when(y_out)
            def _():
                y_copy(kvb.at[0, 2, blk], 2, blk).start()

        zq_copy(qb.at[xl, 1 - zp, blk], blk).wait_recv()
        xq_copy(qb.at[xl, 1 - zp, blk], 1, blk).start()

    prepare_queries(xl, 1 - zp)
    for which in range(2):
        for blk in range(2):
            xq_copy(qb.at[xl, zp, blk], which, blk).wait_recv()
    prepare_queries(1 - xl, zp)
    prepare_queries(1 - xl, 1 - zp)

    def prepare_keys(line, unit):
        index = 3 * line + unit
        parts = []
        for blk in range(2):
            k1, k2, k3 = thirds(kvb[line, unit, blk, 0])
            v1, v2 = halves(kvb[line, unit, blk, 1])
            for i, part in enumerate((k1, k2, k1, k2, k1, k3)):
                kp[index, blk * CELLS:(blk + 1) * CELLS, i * DIM:(i + 1) * DIM] = part
            parts.append(jnp.concatenate([v1, v2, v1, v2], axis=1))
        return jnp.concatenate(parts, axis=0)

    def forward_block(index, values, line_index, half):
        scores = dot(kp[line_index], rq[half], ((1,), (1,)))
        dprobs = dot(values, ro[half], ((1,), (1,)))
        peak = jnp.max(scores, axis=0, keepdims=True)
        weights = jnp.exp(scores - peak)
        wbuf[index] = weights
        dbuf[index] = dprobs
        st[index, 0:1] = peak
        st[index, 1:2] = jnp.sum(weights, axis=0, keepdims=True)
        st[index, 2:3] = jnp.sum(weights * dprobs, axis=0, keepdims=True)

    def empty_stats(index):
        st[index, 0:1] = jnp.full((1, HALF), LOW, F32)
        st[index, 1:3] = jnp.zeros((2, HALF), F32)

    def own_unit(unit, carry):
        @pl.when((unit == 0) | side_in)
        def _():
            values = prepare_keys(0, unit)

            def one(half, c):
                forward_block(3 * unit + half, values, unit, half)
                return c

            lax.fori_loop(0, 2, one, 0)

        @pl.when((unit > 0) & jnp.logical_not(side_in))
        def _():
            empty_stats(3 * unit)
            empty_stats(3 * unit + 1)

        return carry

    lax.fori_loop(0, 3, own_unit, 0)

    def halo_unit(unit, carry):
        valid = y_in & ((unit == 0) | side_in)

        @pl.when(valid)
        def _():
            for blk in range(2):
                y_copy(kvb.at[1, unit, blk], unit, blk).wait_recv()
            values = prepare_keys(1, unit)
            forward_block(3 * unit + 2, values, 3 + unit, 1 - xl)

        @pl.when(jnp.logical_not(valid))
        def _():
            empty_stats(3 * unit + 2)

        return carry

    lax.fori_loop(0, 3, halo_unit, 0)

    me = 2 * xl + zp
    for half in range(2):
        mine = half == 1 - xl
        peaks, sums, centers = [], [], []
        for unit in range(3):
            peaks.append(st[3 * unit + half, 0:1])
            sums.append(st[3 * unit + half, 1:2])
            centers.append(st[3 * unit + half, 2:3])
            peaks.append(jnp.where(mine, st[3 * unit + 2, 0:1], LOW))
            sums.append(jnp.where(mine, st[3 * unit + 2, 1:2], 0.0))
            centers.append(jnp.where(mine, st[3 * unit + 2, 2:3], 0.0))
        peak = peaks[0]
        for p in peaks[1:]:
            peak = jnp.maximum(peak, p)
        total = jnp.zeros_like(peak)
        center = jnp.zeros_like(peak)
        for p, s, c in zip(peaks, sums, centers):
            factor = jnp.exp(p - peak)
            total += s * factor
            center += c * factor
        sall[me, 3 * half:3 * half + 1] = peak
        sall[me, 3 * half + 1:3 * half + 2] = total
        sall[me, 3 * half + 2:3 * half + 3] = center
    sall[me, 6:8] = jnp.zeros((2, HALF), F32)

    def stat_copy(which):
        device = (xpair, zpair, diag)[which]
        return remote(sall.at[me], sall.at[me], stat_sem, (which,), device)

    for which in range(3):
        stat_copy(which).start()
    for which in range(3):
        stat_copy(which).wait_recv()
    for half in range(2):
        peak = sall[0, 3 * half:3 * half + 1]
        for i in range(1, 4):
            peak = jnp.maximum(peak, sall[i, 3 * half:3 * half + 1])
        total = jnp.zeros_like(peak)
        center = jnp.zeros_like(peak)
        for i in range(4):
            factor = jnp.exp(sall[i, 3 * half:3 * half + 1] - peak)
            total += sall[i, 3 * half + 1:3 * half + 2] * factor
            center += sall[i, 3 * half + 2:3 * half + 3] * factor
        inverse = 1.0 / total
        gst[half, 0:1] = peak
        gst[half, 1:2] = inverse
        gst[half, 2:3] = center * inverse

    def backward_block(index, line_index, half):
        alpha = jnp.exp(st[index, 0:1] - gst[half, 0:1]) * gst[half, 1:2]
        probs = wbuf[index] * alpha
        dscores = probs * (dbuf[index] - gst[half, 2:3])
        p1, p2 = halves(probs)
        s1, s2 = halves(dscores)
        q12 = rq[half, :, DIM:3 * DIM]
        o12 = ro[half, :, DIM:3 * DIM]
        k12 = kp[line_index, :, 0:2 * DIM]
        dv = dot(p1, o12, ((1,), (0,))) + dot(p2, o12, ((1,), (0,)))
        dk = dot(s1, q12, ((1,), (0,))) + dot(s2, q12, ((1,), (0,)))
        dq = dot(k12, s1, ((0,), (0,))) + dot(k12, s2, ((0,), (0,)))
        dq = dq[:DIM] + dq[DIM:]
        dqt[half, 0] += dq[:, :UNIT]
        dqt[half, 1] += dq[:, UNIT:]
        return dk[:, :DIM] + dk[:, DIM:], dv[:, :DIM] + dv[:, DIM:]

    def yr_copy(unit):
        return remote(halo.at[unit], yret.at[unit], yr_sem, (unit,), y_from)

    def halo_back(step, carry):
        unit = 2 - step

        @pl.when(y_in & ((unit == 0) | side_in))
        def _():
            dk, dv = backward_block(3 * unit + 2, 3 + unit, 1 - xl)
            halo[unit, 0] = dk
            halo[unit, 1] = dv
            yr_copy(unit).start()

        return carry

    lax.fori_loop(0, 3, halo_back, 0)

    def own_back(step, carry):
        unit = 2 - step

        @pl.when((unit == 0) | side_in)
        def _():
            own[unit] = jnp.zeros((2, UNIT, DIM), F32)

            def one(half, c):
                dk, dv = backward_block(3 * unit + half, unit, half)
                own[unit, 0] += dk
                own[unit, 1] += dv
                return c

            lax.fori_loop(0, 2, one, 0)

        return carry

    lax.fori_loop(0, 3, own_back, 0)

    def dq_copy(which):
        device = (xpair, zpair, diag)[which]
        src = (dqt.at[1 - xl, zp], dqt.at[xl, 1 - zp], dqt.at[1 - xl, 1 - zp])[which]
        return remote(src, dqr.at[which], dq_sem, (which,), device)

    for which in range(3):
        dq_copy(which).start()

    def zr_copy(which):
        return remote(own.at[1 + which], zret.at[which], zr_sem, (which,), (near_id, far_from)[which])

    for which in (1, 0):
        @pl.when(side_in)
        def _():
            @pl.when(y_out)
            def _():
                yr_copy(1 + which).wait_recv()
                own[1 + which] += yret[1 + which]

            zr_copy(which).start()

    for which in range(3):
        dq_copy(which).wait_recv()
    dq = dqt[xl, zp] + dqr[0] + dqr[1] + dqr[2]
    dq = dq.T * SCALE
    fin[0, 0] = dq[:CELLS]
    fin[0, 1] = dq[CELLS:]

    @pl.when(y_out)
    def _():
        yr_copy(0).wait_recv()
        own[0] += yret[0]

    @pl.when(far_out)
    def _():
        zr_copy(1).wait_recv()
        own[0] += zret[1]

    @pl.when(side_in)
    def _():
        zr_copy(0).wait_recv()
        own[0] += zret[0]

    for i in range(2):
        for blk in range(2):
            fin[1 + i, blk] = own[0, i, blk * CELLS:(blk + 1) * CELLS]

    final = remote(fin.at[:, 1 - core], fout, fin_sem, (0,), sib_id)
    final.start()
    lanes = pl.ds(pl.multiple_of(core * DIM, DIM), DIM)
    other = pl.ds(pl.multiple_of((1 - core) * DIM, DIM), DIM)
    for i in range(3):
        out_ref[i, :, lanes] = fin[i, core]
    final.wait_recv()
    for i in range(3):
        out_ref[i, :, other] = fout[i]

    final.wait_send()
    core_copy().wait_send()
    for blk in range(2):
        @pl.when(y_out)
        def _():
            y_copy(sib.at[pl.ds(0, 2)], 0, blk).wait_send()

            @pl.when(side_in)
            def _():
                for unit in (1, 2):
                    y_copy(kvb.at[0, unit, blk], unit, blk).wait_send()

        @pl.when(side_in)
        def _():
            near_copy(sib.at[pl.ds(0, 2)], blk).wait_send()

        @pl.when(far_out)
        def _():
            far_copy(sib.at[pl.ds(0, 2)], blk).wait_send()

        zq_copy(sib.at[pl.ds(2, 2)], blk).wait_send()
        for which in range(2):
            xq_copy(sib.at[pl.ds(2, 2)], which, blk).wait_send()
    for which in range(3):
        stat_copy(which).wait_send()
        dq_copy(which).wait_send()

    @pl.when(y_in)
    def _():
        yr_copy(0).wait_send()

    @pl.when(side_in)
    def _():
        for which in range(2):
            zr_copy(which).wait_send()

            @pl.when(y_in)
            def _():
                yr_copy(1 + which).wait_send()


def body(query_field, key_field, value_field, output_grad):
    frames, rows, cols, channels = query_field.shape
    packed = jnp.stack([key_field, value_field, query_field, output_grad])
    packed = packed.reshape(4, CELLS, 2, DIM).transpose(2, 0, 1, 3)

    def sems(*shape):
        return pltpu.SemaphoreType.DMA((2,) + shape)

    out = pl.pallas_call(
        kernel,
        out_shape=jax.ShapeDtypeStruct((3, CELLS, channels), F32),
        in_specs=[pl.BlockSpec(memory_space=pltpu.VMEM)],
        out_specs=pl.BlockSpec(memory_space=pltpu.VMEM),
        scratch_shapes=[
            pltpu.VMEM((4, CELLS, DIM), F32),
            pltpu.VMEM((2, 3, 2, 2, CELLS, DIM), F32),
            pltpu.VMEM((2, 2, 2, 2, CELLS, DIM), F32),
            pltpu.VMEM((6, UNIT, 6 * DIM), BF16),
            pltpu.VMEM((2, HALF, 6 * DIM), BF16),
            pltpu.VMEM((2, HALF, 4 * DIM), BF16),
            pltpu.VMEM((9, UNIT, HALF), F32),
            pltpu.VMEM((9, UNIT, HALF), F32),
            pltpu.VMEM((9, 8, HALF), F32),
            pltpu.VMEM((4, 8, HALF), F32),
            pltpu.VMEM((2, 8, HALF), F32),
            pltpu.VMEM((2, 2, DIM, UNIT), F32),
            pltpu.VMEM((3, DIM, UNIT), F32),
            pltpu.VMEM((3, 2, UNIT, DIM), F32),
            pltpu.VMEM((3, 2, UNIT, DIM), F32),
            pltpu.VMEM((3, 2, UNIT, DIM), F32),
            pltpu.VMEM((2, 2, UNIT, DIM), F32),
            pltpu.VMEM((3, 2, CELLS, DIM), F32),
            pltpu.VMEM((3, CELLS, DIM), F32),
            sems(1), sems(2), sems(2), sems(3, 2), sems(2), sems(2, 2), sems(3), sems(3), sems(2), sems(3), sems(1),
        ],
        compiler_params=pltpu.CompilerParams(
            collective_id=0, has_side_effects=True, vmem_limit_bytes=56 * 1024 * 1024
        ),
    )(packed)
    out = out.reshape(3, frames, rows, cols, channels)
    return out[0], out[1], out[2]


def solution(mesh):
    spec = P(None, "ha", "wa", None)
    return jax.shard_map(
        body, mesh=mesh, in_specs=(spec,) * 4, out_specs=(spec,) * 3, check_vma=False,
    )
```

time: 671 us -> 69.2 us (0.10)
  the two profiles are of different devices: /device:TPU:53 before, /device:TPU:14 now
where the time goes in v1:
time: 69.2 us; the launch traced here: 68.4 us
  Pallas kernels  59.7 us (86%)
  local copies, waits for them, and re-layouts  7.12 us (10%)
  other arithmetic  0.84 us (1%)
  between operations  0.71 us (1%)
    pallas_call x1, Pallas kernels, body(): pl.pallas_call(kernel, out_shape=jax.ShapeDtypeStruct((3, CELLS, channels...  59.7 us
    unnamed x6, local copies, waits for them, and re-layouts  2.64 us
    squeeze x3, local copies, waits for them, and re-layouts, body(): return (out[0], out[1], out[2])  2.08 us

profile of v1, /device:TPU:14, one launch (start us, length us, event | category | flops | bytes accessed | tf_op | source)
XLA Modules:
  0.0 68.4 jit_solution(3918493319844696390)
XLA Ops:
  0.6 1.0 %stack.17 = f32[1,128,2,128]{3,2,1,0:T(2,128)S(1)} reshape(f32[2,16,4,256]{3,2,1,0:T(4,128)} %param.4) | data formatting | bytes 262144 | tf_op jit(solution)/shard_map/stack | solution.py:425
  1.6 0.0 copy-start
  1.7 0.9 %copy-done = f32[2,16,4,256]{3,2,1,0:T(4,128)S(1)} copy-done((f32[2,16,4,256]{3,2,1,0:T(4,128)S(1)}, f32[2,16,4,256]{3,2,1,0:T(4,128)}, u32[]{:S(2)}) %copy-start) | copy-done | bytes 131096
  2.5 0.1 stack.15
  2.6 0.0 copy-start.1
  2.7 0.9 %copy-done.1 = f32[2,16,4,256]{3,2,1,0:T(4,128)S(1)} copy-done((f32[2,16,4,256]{3,2,1,0:T(4,128)S(1)}, f32[2,16,4,256]{3,2,1,0:T(4,128)}, u32[]{:S(2)}) %copy-start.1) | copy-done | bytes 131096
  3.6 0.1 stack.16
  3.7 0.0 copy-start.2
  3.7 0.9 %copy-done.2 = f32[2,16,4,256]{3,2,1,0:T(4,128)S(1)} copy-done((f32[2,16,4,256]{3,2,1,0:T(4,128)S(1)}, f32[2,16,4,256]{3,2,1,0:T(4,128)}, u32[]{:S(2)}) %copy-start.2) | copy-done | bytes 131096
  4.6 0.1 stack.18
  4.7 0.8 %maximum_bitcast_fusion.x_ref = f32[2,4,128,128]{3,2,1,0:T(8,128)} fusion(f32[1,128,2,128]{3,1,0,2:T(8,128)S(1)} %copy.10, f32[1,128,2,128]{3,1,0,2:T(8,128)S(1)} %copy.9, f32[1,128,2,128]{3,1,0,2:T(8,128)S(1)} %copy.8, f32[1,128,2,128]{3,1,0,2:T(8,128)S(1)} %copy.7), kind=kLoop, calls=%fused_computation | loop fusion | flops 393216 | bytes 1048576 | tf_op jit(solution)/shard_map/transpose | solution.py:426
  5.5 59.7 %shard_map.67 = f32[3,128,256]{2,1,0:T(8,128)} custom-call(f32[2,4,128,128]{3,2,1,0:T(8,128)} %maximum_bitcast_fusion.x_ref), custom_call_target="tpu_custom_call" | custom-call | tf_op jit(solution)/shard_map/pallas_call | solution.py:431
  65.2 1.1 %fusion = (f32[1,128,256]{2,1,0:T(8,128)S(1)}, f32[1,128,256]{2,1,0:T(8,128)S(1)}, f32[1,128,256]{2,1,0:T(8,128)S(1)}) fusion(f32[3,128,256]{2,1,0:T(8,128)} %shard_map.67), kind=kLoop, calls=%fused_computation.1 | loop fusion | bytes 786432 | tf_op jit(solution)/shard_map/slice | solution.py:463
  66.3 0.7 %squeeze.11 = f32[2,16,4,256]{3,2,1,0:T(4,128)} reshape(f32[1,128,256]{2,1,0:T(8,128)S(1)} %get-tuple-element.3) | data formatting | bytes 262144 | tf_op jit(solution)/shard_map/squeeze | solution.py:463
  67.0 0.7 %squeeze.10 = f32[2,16,4,256]{3,2,1,0:T(4,128)} reshape(f32[1,128,256]{2,1,0:T(8,128)S(1)} %get-tuple-element.4) | data formatting | bytes 262144 | tf_op jit(solution)/shard_map/squeeze | solution.py:463
  67.7 0.7 %squeeze.9 = f32[2,16,4,256]{3,2,1,0:T(4,128)} reshape(f32[1,128,256]{2,1,0:T(8,128)S(1)} %get-tuple-element.5) | data formatting | bytes 262144 | tf_op jit(solution)/shard_map/squeeze | solution.py:463
  (4 shorter events, 0.0 us)
Async XLA Ops:
  1.6 0.9 %copy-start = (f32[2,16,4,256]{3,2,1,0:T(4,128)S(1)}, f32[2,16,4,256]{3,2,1,0:T(4,128)}, u32[]{:S(2)}) copy-start(f32[2,16,4,256]{3,2,1,0:T(4,128)} %param.5) | copy-start | bytes 393220
  2.6 0.9 %copy-start.1 = (f32[2,16,4,256]{3,2,1,0:T(4,128)S(1)}, f32[2,16,4,256]{3,2,1,0:T(4,128)}, u32[]{:S(2)}) copy-start(f32[2,16,4,256]{3,2,1,0:T(4,128)} %param.6) | copy-start | bytes 393220
  3.7 0.9 %copy-start.2 = (f32[2,16,4,256]{3,2,1,0:T(4,128)S(1)}, f32[2,16,4,256]{3,2,1,0:T(4,128)}, u32[]{:S(2)}) copy-start(f32[2,16,4,256]{3,2,1,0:T(4,128)} %param.7) | copy-start | bytes 393220

commit v2 on v0

v2 whole, which is shorter than its diff:
```python
import jax
import jax.numpy as jnp
from jax import lax
from jax.experimental import pallas as pl
from jax.experimental.pallas import tpu as pltpu
from jax.sharding import PartitionSpec as P

MESH = pl.DeviceIdType.MESH
F32 = jnp.float32
BF16 = jnp.bfloat16
DIM = 128
SCALE = DIM ** -0.5
LOW = -1e30
CELLS = 128
KEYS = 3 * CELLS
HALF = 4 * CELLS


def halves(x):
    hi = x.astype(BF16)
    return hi, (x - hi.astype(F32)).astype(BF16)


def thirds(x):
    hi = x.astype(BF16)
    rest = x - hi.astype(F32)
    mid = rest.astype(BF16)
    return hi, mid, (rest - mid.astype(F32)).astype(BF16)


def dot(a, b, dims):
    return lax.dot_general(a, b, (dims, ((), ())), preferred_element_type=F32)


def kernel(
    q_in, k_in, v_in, g_in, dq_out, dk_out, dv_out,
    raw, kvb, qb, kp, lv, rq, ro, wbuf, dbuf, st, sst, sall, gst, dqt, dqs, dqr, own, halo, yret, zret,
    in_sem, near_sem, far_sem, y_sem, zq_sem, xq_sem, diag_sem, sibq_sem, pair_sem, stat_sem,
    yr_sem, zr_sem, dqs_sem, dq_sem,
):
    ha, wa = lax.axis_index("ha"), lax.axis_index("wa")
    row, xl = ha // 2, ha % 2
    core = wa % 2
    chip = wa // 2
    zp = chip % 2
    tile = chip // 2
    side = 2 * zp - 1
    up = 2 * xl - 1

    sib_id = (ha, wa + 1 - 2 * core)
    near_id = (ha, (wa + 2 * side + 32) % 32)
    far_to = (ha, (wa - 4 * side + 32) % 32)
    far_from = (ha, (wa + 4 * side + 32) % 32)
    zpair = (ha, wa - 2 * side)
    xpair = (ha - up, wa)
    diag = (ha - up, wa - 2 * side)
    y_to = ((ha + 2 * up + 8) % 8, wa)
    y_from = ((ha - 2 * up + 8) % 8, wa)

    side_in = jnp.where(zp == 0, tile > 0, tile < 7)
    far_out = jnp.where(zp == 0, tile < 7, tile > 0)
    y_out = jnp.where(xl == 1, row < 3, row > 0)
    y_in = jnp.where(xl == 1, row > 0, row < 3)
    z_first = (tile > 0) & (tile < 7)

    barrier = pltpu.get_barrier_semaphore()
    partners = (sib_id, near_id, far_to, far_from, zpair, xpair, diag, y_to, y_from)
    for device in partners:
        pl.semaphore_signal(barrier, inc=1, device_id=device, device_id_type=MESH)
    loads = [
        pltpu.make_async_copy(ref, raw.at[i], in_sem.at[i]) for i, ref in enumerate((k_in, v_in, q_in, g_in))
    ]
    for load in loads:
        load.start()
    for load in loads:
        load.wait()
    for h in range(2):
        for i in range(4):
            part = raw[i, :, :, h * DIM:(h + 1) * DIM].reshape(CELLS, DIM)
            if i < 2:
                kvb[h, 0, 0, i] = part
            else:
                qb[h, xl, zp, core, i - 2] = part
    pl.semaphore_wait(barrier, len(partners))

    def remote(src, dst, sems, index, device):
        return pltpu.make_async_remote_copy(
            src_ref=src, dst_ref=dst, send_sem=sems.at[(0,) + index], recv_sem=sems.at[(1,) + index],
            device_id=device, device_id_type=MESH,
        )

    def near_copy(h):
        return remote(kvb.at[h, 0, 0], kvb.at[h, 0, 1], near_sem, (h,), near_id)

    def far_copy(h):
        return remote(kvb.at[h, 0, 0], kvb.at[h, 0, 2], far_sem, (h,), far_to)

    def y_copy(h, unit):
        return remote(kvb.at[h, 0, unit], kvb.at[h, 1, unit], y_sem, (h, unit), y_to)

    def q_copy(h, half, place, sems, device):
        return remote(qb.at[h, half, place, core], qb.at[h, half, place, core], sems, (h,), device)

    def zq_copy(h):
        return q_copy(h, xl, zp, zq_sem, zpair)

    def xq_copy(h):
        return q_copy(h, xl, zp, xq_sem, xpair)

    def diag_by_x(h):
        return q_copy(h, xl, 1 - zp, diag_sem, xpair)

    def diag_by_z(h):
        return q_copy(h, 1 - xl, zp, diag_sem, zpair)

    def sib_copy(h, slot):
        half, place = (
            (xl, zp), (xl, 1 - zp), (1 - xl, zp), (1 - xl, 1 - zp)
        )[slot]
        block = qb.at[h, half, place, core]
        return remote(block, block, sibq_sem, (h, slot), sib_id)

    def first_sends(h):
        @pl.when(y_out)
        def _():
            y_copy(h, 0).start()

        @pl.when(side_in)
        def _():
            near_copy(h).start()

        @pl.when(far_out)
        def _():
            far_copy(h).start()

        zq_copy(h).start()
        xq_copy(h).start()
        sib_copy(h, 0).start()

    def pass_on(h):
        @pl.when(side_in)
        def _():
            near_copy(h).wait_recv()

            @pl.when(y_out)
            def _():
                y_copy(h, 1).start()

            far_copy(h).wait_recv()

            @pl.when(y_out)
            def _():
                y_copy(h, 2).start()

        zq_copy(h).wait_recv()
        sib_copy(h, 1).start()

        @pl.when(z_first)
        def _():
            diag_by_x(h).start()

        xq_copy(h).wait_recv()
        sib_copy(h, 2).start()

        @pl.when(jnp.logical_not(z_first))
        def _():
            diag_by_z(h).start()

    def last_queries(h):
        diag_by_x(h).wait_recv()
        sib_copy(h, 3).start()

    def prepare_queries(h):
        for slot in range(4):
            sib_copy(h, slot).wait_recv()

        def one(index, c):
            half, place = index // 2, index % 2
            for blk in range(2):
                q1, q2, q3 = thirds(qb[h, half, place, blk, 0] * SCALE)
                o1, o2 = halves(qb[h, half, place, blk, 1])
                rows = pl.ds(pl.multiple_of(place * (2 * CELLS) + blk * CELLS, CELLS), CELLS)
                for i, part in enumerate((q1, q1, q2, q2, q3, q1)):
                    rq[h, half, rows, i * DIM:(i + 1) * DIM] = part
                for i, part in enumerate((o1, o1, o2, o2)):
                    ro[h, half, rows, i * DIM:(i + 1) * DIM] = part
            return c

        lax.fori_loop(0, 4, one, 0)

    def prepare_keys(h, line):
        for unit in range(3):
            rows = slice(unit * CELLS, (unit + 1) * CELLS)
            k1, k2, k3 = thirds(kvb[h, line, unit, 0])
            v1, v2 = halves(kvb[h, line, unit, 1])
            for i, part in enumerate((k1, k2, k1, k2, k1, k3)):
                kp[2 * h + line, rows, i * DIM:(i + 1) * DIM] = part
            for i, part in enumerate((v1, v2, v1, v2)):
                lv[rows, i * DIM:(i + 1) * DIM] = part

    far_keys = lax.broadcasted_iota(jnp.int32, (KEYS, 1), 0) >= CELLS
    bias = jnp.where(far_keys, jnp.where(side_in, 0.0, LOW), 0.0)

    def forward_block(h, k, line, half):
        index = 3 * h + k
        scores = dot(kp[2 * h + line], rq[h, half], ((1,), (1,))) + bias
        dprobs = dot(lv[...], ro[h, half], ((1,), (1,)))
        peak = jnp.max(scores, axis=0, keepdims=True)
        weights = jnp.exp(scores - peak)
        wbuf[index] = weights
        dbuf[index] = dprobs
        st[index, 0:1] = peak
        st[index, 1:2] = jnp.sum(weights, axis=0, keepdims=True)
        st[index, 2:3] = jnp.sum(weights * dprobs, axis=0, keepdims=True)

    def own_forward(h):
        prepare_keys(h, 0)

        def one(half, c):
            forward_block(h, half, 0, half)
            return c

        lax.fori_loop(0, 2, one, 0)

    def halo_forward(h):
        @pl.when(y_in)
        def _():
            y_copy(h, 0).wait_recv()

            @pl.when(side_in)
            def _():
                y_copy(h, 1).wait_recv()
                y_copy(h, 2).wait_recv()

            prepare_keys(h, 1)
            forward_block(h, 2, 1, 1 - xl)

        @pl.when(jnp.logical_not(y_in))
        def _():
            st[3 * h + 2, 0:1] = jnp.full((1, HALF), LOW, F32)
            st[3 * h + 2, 1:3] = jnp.zeros((2, HALF), F32)

    me = 2 * xl + zp

    def merge(triples):
        peak = triples[0][0]
        for p, _, _ in triples[1:]:
            peak = jnp.maximum(peak, p)
        total = jnp.zeros_like(peak)
        center = jnp.zeros_like(peak)
        for p, s, c in triples:
            factor = jnp.exp(p - peak)
            total += s * factor
            center += c * factor
        return peak, total, center

    def triple(ref, base):
        return tuple(ref[base + i:base + i + 1] for i in range(3))

    def pair_copy(h):
        return remote(sst.at[h, core], sst.at[h, core], pair_sem, (h,), sib_id)

    def stat_copy(h, which):
        device = (xpair, zpair, diag)[which]
        return remote(sall.at[h, me], sall.at[h, me], stat_sem, (h, which), device)

    def start_stats(h):
        for half in range(2):
            mine = half == 1 - xl
            extra = triple(st.at[3 * h + 2], 0)
            extra = (
                jnp.where(mine, extra[0], LOW), jnp.where(mine, extra[1], 0.0), jnp.where(mine, extra[2], 0.0)
            )
            merged = merge([triple(st.at[3 * h + half], 0), extra])
            for i in range(3):
                sst[h, core, 3 * half + i:3 * half + i + 1] = merged[i]
        sst[h, core, 6:8] = jnp.zeros((2, HALF), F32)
        pair_copy(h).start()

    def share_stats(h):
        pair_copy(h).wait_recv()
        for half in range(2):
            merged = merge([triple(sst.at[h, i], 3 * half) for i in range(2)])
            for i in range(3):
                sall[h, me, 3 * half + i:3 * half + i + 1] = merged[i]
        sall[h, me, 6:8] = jnp.zeros((2, HALF), F32)
        for which in range(3):
            stat_copy(h, which).start()

    def end_stats(h):
        for which in range(3):
            stat_copy(h, which).wait_recv()
        for half in range(2):
            peak, total, center = merge([triple(sall.at[h, i], 3 * half) for i in range(4)])
            inverse = 1.0 / total
            gst[h, half, 0:1] = peak
            gst[h, half, 1:2] = inverse
            gst[h, half, 2:3] = center * inverse

    def backward_block(h, k, line, half):
        index = 3 * h + k
        alpha = jnp.exp(st[index, 0:1] - gst[h, half, 0:1]) * gst[h, half, 1:2]
        probs = wbuf[index] * alpha
        dscores = probs * (dbuf[index] - gst[h, half, 2:3])
        p1, p2 = halves(probs)
        s1, s2 = halves(dscores)
        q12 = rq[h, half, :, DIM:3 * DIM]
        o12 = ro[h, half, :, DIM:3 * DIM]
        k12 = kp[2 * h + line, :, 0:2 * DIM]
        dv = dot(p1, o12, ((1,), (0,))) + dot(p2, o12, ((1,), (0,)))
        dk = dot(s1, q12, ((1,), (0,))) + dot(s2, q12, ((1,), (0,)))
        dq = dot(k12, s1, ((0,), (0,))) + dot(k12, s2, ((0,), (0,)))
        dq = dq[:DIM] + dq[DIM:]
        for place in range(2):
            for blk in range(2):
                at = (2 * place + blk) * CELLS
                dqt[h, half, place, blk] += dq[:, at:at + CELLS]
        return dk[:, :DIM] + dk[:, DIM:], dv[:, :DIM] + dv[:, DIM:]

    def yr_copy(h, unit):
        return remote(halo.at[h, unit], yret.at[h, unit], yr_sem, (h, unit), y_from)

    def dqs_copy(h):
        return remote(dqt.at[h, :, :, 1 - core], dqs.at[h], dqs_sem, (h,), sib_id)

    def backward(h):
        dqt[h] = jnp.zeros(dqt.shape[1:], F32)
        own[h] = jnp.zeros(own.shape[1:], F32)

        @pl.when(y_in)
        def _():
            dk, dv = backward_block(h, 2, 1, 1 - xl)
            for unit in range(3):
                halo[h, unit, 0] = dk[unit * CELLS:(unit + 1) * CELLS]
                halo[h, unit, 1] = dv[unit * CELLS:(unit + 1) * CELLS]

            @pl.when(side_in)
            def _():
                yr_copy(h, 2).start()
                yr_copy(h, 1).start()

            yr_copy(h, 0).start()

        def one(half, c):
            dk, dv = backward_block(h, half, 0, half)
            for unit in range(3):
                own[h, unit, 0] += dk[unit * CELLS:(unit + 1) * CELLS]
                own[h, unit, 1] += dv[unit * CELLS:(unit + 1) * CELLS]
            return c

        lax.fori_loop(0, 2, one, 0)
        dqs_copy(h).start()

    def dq_copy(h, which):
        device = (xpair, zpair, diag)[which]
        half, place = ((1 - xl, zp), (xl, 1 - zp), (1 - xl, 1 - zp))[which]
        return remote(dqt.at[h, half, place, core], dqr.at[h, which], dq_sem, (h, which), device)

    def share_dq(h):
        dqs_copy(h).wait_recv()
        for half in range(2):
            for place in range(2):
                dqt[h, half, place, core] += dqs[h, half, place]
        for which in range(3):
            dq_copy(h, which).start()

    def zr_copy(h, which):
        return remote(own.at[h, 1 + which], zret.at[h, which], zr_sem, (h, which), (near_id, far_from)[which])

    def pass_back(h):
        for which in (1, 0):
            @pl.when(side_in)
            def _():
                @pl.when(y_out)
                def _():
                    yr_copy(h, 1 + which).wait_recv()
                    own[h, 1 + which] += yret[h, 1 + which]

                zr_copy(h, which).start()

    def finish(h):
        lanes = slice(h * DIM, (h + 1) * DIM)
        for which in range(3):
            dq_copy(h, which).wait_recv()
        dq = dqt[h, xl, zp, core] + dqr[h, 0] + dqr[h, 1] + dqr[h, 2]
        dq_out[:, :, lanes] = (dq.T * SCALE).reshape(32, 4, DIM)

        @pl.when(y_out)
        def _():
            yr_copy(h, 0).wait_recv()
            own[h, 0] += yret[h, 0]

        @pl.when(far_out)
        def _():
            zr_copy(h, 1).wait_recv()
            own[h, 0] += zret[h, 1]

        @pl.when(side_in)
        def _():
            zr_copy(h, 0).wait_recv()
            own[h, 0] += zret[h, 0]

        dk_out[:, :, lanes] = own[h, 0, 0].reshape(32, 4, DIM)
        dv_out[:, :, lanes] = own[h, 0, 1].reshape(32, 4, DIM)

    def all_left(h):
        @pl.when(y_out)
        def _():
            y_copy(h, 0).wait_send()

            @pl.when(side_in)
            def _():
                y_copy(h, 1).wait_send()
                y_copy(h, 2).wait_send()

        @pl.when(side_in)
        def _():
            near_copy(h).wait_send()
            for which in range(2):
                zr_copy(h, which).wait_send()

        @pl.when(far_out)
        def _():
            far_copy(h).wait_send()

        @pl.when(y_in)
        def _():
            yr_copy(h, 0).wait_send()

            @pl.when(side_in)
            def _():
                yr_copy(h, 1).wait_send()
                yr_copy(h, 2).wait_send()

        zq_copy(h).wait_send()
        xq_copy(h).wait_send()
        diag_by_x(h).wait_send()
        for slot in range(4):
            sib_copy(h, slot).wait_send()
        pair_copy(h).wait_send()
        dqs_copy(h).wait_send()
        for which in range(3):
            stat_copy(h, which).wait_send()
            dq_copy(h, which).wait_send()

    first_sends(0)

    @pl.when(jnp.logical_not(side_in))
    def _():
        for h in range(2):
            for line in range(2):
                kvb[h, line, 1:3] = jnp.zeros((2, 2, CELLS, DIM), F32)

    pass_on(0)
    first_sends(1)
    last_queries(0)
    prepare_queries(0)
    own_forward(0)
    pass_on(1)
    halo_forward(0)
    start_stats(0)
    last_queries(1)
    share_stats(0)
    prepare_queries(1)
    own_forward(1)
    end_stats(0)
    backward(0)
    halo_forward(1)
    start_stats(1)
    share_dq(0)
    share_stats(1)
    pass_back(0)
    end_stats(1)
    backward(1)
    finish(0)
    share_dq(1)
    pass_back(1)
    finish(1)
    all_left(0)
    all_left(1)


def body(query_field, key_field, value_field, output_grad):
    frames, rows, cols, channels = query_field.shape
    flat = (frames * rows, cols, channels)

    def sems(*shape):
        return pltpu.SemaphoreType.DMA((2, 2) + shape)

    outs = pl.pallas_call(
        kernel,
        out_shape=[jax.ShapeDtypeStruct(flat, F32)] * 3,
        in_specs=[pl.BlockSpec(memory_space=pl.ANY)] * 4,
        out_specs=[pl.BlockSpec(memory_space=pltpu.VMEM)] * 3,
        scratch_shapes=[
            pltpu.VMEM((4,) + flat, F32),
            pltpu.VMEM((2, 2, 3, 2, CELLS, DIM), F32),
            pltpu.VMEM((2, 2, 2, 2, 2, CELLS, DIM), F32),
            pltpu.VMEM((4, KEYS, 6 * DIM), BF16),
            pltpu.VMEM((KEYS, 4 * DIM), BF16),
            pltpu.VMEM((2, 2, HALF, 6 * DIM), BF16),
            pltpu.VMEM((2, 2, HALF, 4 * DIM), BF16),
            pltpu.VMEM((6, KEYS, HALF), F32),
            pltpu.VMEM((6, KEYS, HALF), F32),
            pltpu.VMEM((6, 8, HALF), F32),
            pltpu.VMEM((2, 2, 8, HALF), F32),
            pltpu.VMEM((2, 4, 8, HALF), F32),
            pltpu.VMEM((2, 2, 8, HALF), F32),
            pltpu.VMEM((2, 2, 2, 2, DIM, CELLS), F32),
            pltpu.VMEM((2, 2, 2, DIM, CELLS), F32),
            pltpu.VMEM((2, 3, DIM, CELLS), F32),
            pltpu.VMEM((2, 3, 2, CELLS, DIM), F32),
            pltpu.VMEM((2, 3, 2, CELLS, DIM), F32),
            pltpu.VMEM((2, 3, 2, CELLS, DIM), F32),
            pltpu.VMEM((2, 2, 2, CELLS, DIM), F32),
            pltpu.SemaphoreType.DMA((4,)),
            sems(), sems(), sems(3), sems(), sems(), sems(), sems(4), sems(), sems(3),
            sems(3), sems(2), sems(), sems(3),
        ],
        compiler_params=pltpu.CompilerParams(
            collective_id=0, has_side_effects=True, vmem_limit_bytes=56 * 1024 * 1024
        ),
    )(*(x.reshape(flat) for x in (query_field, key_field, value_field, output_grad)))
    return tuple(x.reshape(frames, rows, cols, channels) for x in outs)


def solution(mesh):
    spec = P(None, "ha", "wa", None)
    return jax.shard_map(
        body, mesh=mesh, in_specs=(spec,) * 4, out_specs=(spec,) * 3, check_vma=False,
    )
```

time: 671 us -> 70.7 us (0.11)
  the two profiles are of different devices: /device:TPU:53 before, /device:TPU:1 now
where the time goes in v2:
time: 70.7 us; the launch traced here: 70.6 us
  Pallas kernels  66.7 us (94%)
  local copies, waits for them, and re-layouts  3.21 us (5%)
    pallas_call x1, Pallas kernels, body(): pl.pallas_call(kernel, out_shape=[jax.ShapeDtypeStruct(flat, F32)] * 3, i...  66.7 us
    unnamed x7, local copies, waits for them, and re-layouts  3.21 us

profile of v2, /device:TPU:1, one launch (start us, length us, event | category | flops | bytes accessed | tf_op | source)
XLA Modules:
  0.0 70.6 jit_solution(12471509544516406327)
XLA Ops:
  0.6 66.7 %shard_map.67 = (f32[32,4,256]{2,1,0:T(4,128)}, f32[32,4,256]{2,1,0:T(4,128)}, f32[32,4,256]{2,1,0:T(4,128)}) custom-call(f32[32,4,256]{2,1,0:T(4,128)} %bitcast.10, f32[32,4,256]{2,1,0:T(4,128)} %bitcast.11, f32[32,4,256]{2,1,0:T(4,128)} %bitcast.12, f32[32,4,256]{2,1,0:T(4,128)} %bitcast.13), custom_call_target="tpu_custom_call" | custom-call | tf_op jit(solution)/shard_map/pallas_call | solution.py:490
  67.4 0.0 copy-start.1
  67.4 1.6 %copy.10 = f32[2,16,4,256]{3,2,1,0:T(4,128)} copy(f32[2,16,4,256]{3,2,1,0:T(4,128)} %bitcast.9) | data formatting | bytes 262144
  69.0 0.0 copy-done.1
  69.0 0.0 copy-start
  69.0 0.7 copy.11
  69.6 0.3 copy-done
  69.9 0.7 copy.12
Async XLA Ops:
  67.4 1.6 %copy-start.1 = (f32[32,4,256]{2,1,0:T(4,128)S(1)}, f32[32,4,256]{2,1,0:T(4,128)}, u32[]{:S(2)}) copy-start(f32[32,4,256]{2,1,0:T(4,128)} %get-tuple-element.7) | copy-start | bytes 393220
  69.0 1.0 %copy-start = (f32[32,4,256]{2,1,0:T(4,128)S(1)}, f32[32,4,256]{2,1,0:T(4,128)}, u32[]{:S(2)}) copy-start(f32[32,4,256]{2,1,0:T(4,128)} %get-tuple-element.8) | copy-start | bytes 393220

commit v3 on v2

--- a/solution.py
+++ b/solution.py
@@ -89,93 +89,101 @@
             device_id=device, device_id_type=MESH,
         )
 
-    def near_copy(h):
-        return remote(kvb.at[h, 0, 0], kvb.at[h, 0, 1], near_sem, (h,), near_id)
-
-    def far_copy(h):
-        return remote(kvb.at[h, 0, 0], kvb.at[h, 0, 2], far_sem, (h,), far_to)
-
-    def y_copy(h, unit):
-        return remote(kvb.at[h, 0, unit], kvb.at[h, 1, unit], y_sem, (h, unit), y_to)
-
-    def q_copy(h, half, place, sems, device):
-        return remote(qb.at[h, half, place, core], qb.at[h, half, place, core], sems, (h,), device)
-
-    def zq_copy(h):
-        return q_copy(h, xl, zp, zq_sem, zpair)
-
-    def xq_copy(h):
-        return q_copy(h, xl, zp, xq_sem, xpair)
-
-    def diag_by_x(h):
-        return q_copy(h, xl, 1 - zp, diag_sem, xpair)
-
-    def diag_by_z(h):
-        return q_copy(h, 1 - xl, zp, diag_sem, zpair)
+    def near_copy(h, kv):
+        return remote(kvb.at[h, 0, 0, kv], kvb.at[h, 0, 1, kv], near_sem, (h, kv), near_id)
+
+    def far_copy(h, kv):
+        return remote(kvb.at[h, 0, 0, kv], kvb.at[h, 0, 2, kv], far_sem, (h, kv), far_to)
+
+    def y_copy(h, unit, kv):
+        return remote(kvb.at[h, 0, unit, kv], kvb.at[h, 1, unit, kv], y_sem, (h, unit, kv), y_to)
+
+    def q_copy(h, half, place, part, sems, device):
+        block = qb.at[h, half, place, core, part]
+        return remote(block, block, sems, (h, part), device)
+
+    def zq_copy(h, part):
+        return q_copy(h, xl, zp, part, zq_sem, zpair)
+
+    def xq_copy(h, part):
+        return q_copy(h, xl, zp, part, xq_sem, xpair)
+
+    def diag_by_x(h, part):
+        return q_copy(h, xl, 1 - zp, part, diag_sem, xpair)
+
+    def diag_by_z(h, part):
+        return q_copy(h, 1 - xl, zp, part, diag_sem, zpair)
+
+    def slot_place(slot):
+        return xl + (slot // 2) * (1 - 2 * xl), zp + (slot % 2) * (1 - 2 * zp)
 
     def sib_copy(h, slot):
-        half, place = (
-            (xl, zp), (xl, 1 - zp), (1 - xl, zp), (1 - xl, 1 - zp)
-        )[slot]
+        half, place = slot_place(slot)
         block = qb.at[h, half, place, core]
         return remote(block, block, sibq_sem, (h, slot), sib_id)
 
     def first_sends(h):
         @pl.when(y_out)
         def _():
-            y_copy(h, 0).start()
-
+            y_copy(h, 0, 0).start()
+            y_copy(h, 0, 1).start()
+
+        for part in range(2):
+            @pl.when(side_in)
+            def _():
+                near_copy(h, part).start()
+
+            @pl.when(far_out)
+            def _():
+                far_copy(h, part).start()
+
+            zq_copy(h, part).start()
+            xq_copy(h, part).start()
+        sib_copy(h, 0).start()
+
+    def pass_keys(h, kv):
         @pl.when(side_in)
         def _():
-            near_copy(h).start()
-
-        @pl.when(far_out)
-        def _():
-            far_copy(h).start()
-
-        zq_copy(h).start()
-        xq_copy(h).start()
-        sib_copy(h, 0).start()
-
-    def pass_on(h):
-        @pl.when(side_in)
-        def _():
-            near_copy(h).wait_recv()
+            near_copy(h, kv).wait_recv()
 
             @pl.when(y_out)
             def _():
-                y_copy(h, 1).start()
-
-            far_copy(h).wait_recv()
+                y_copy(h, 1, kv).start()
+
+            far_copy(h, kv).wait_recv()
 
             @pl.when(y_out)
             def _():
-                y_copy(h, 2).start()
-
-        zq_copy(h).wait_recv()
+                y_copy(h, 2, kv).start()
+
+    def pass_queries(h):
+        xq_copy(h, 1).wait_recv()
+        diag_by_z(h, 1).start()
+        zq_copy(h, 0).wait_recv()
+
+        @pl.when(z_first)
+        def _():
+            diag_by_x(h, 0).start()
+
+        xq_copy(h, 0).wait_recv()
+        sib_copy(h, 2).start()
+
+        @pl.when(jnp.logical_not(z_first))
+        def _():
+            diag_by_z(h, 0).start()
+
+        zq_copy(h, 1).wait_recv()
         sib_copy(h, 1).start()
 
-        @pl.when(z_first)
-        def _():
-            diag_by_x(h).start()
-
-        xq_copy(h).wait_recv()
-        sib_copy(h, 2).start()
-
-        @pl.when(jnp.logical_not(z_first))
-        def _():
-            diag_by_z(h).start()
-
     def last_queries(h):
-        diag_by_x(h).wait_recv()
+        for part in range(2):
+            diag_by_x(h, part).wait_recv()
         sib_copy(h, 3).start()
 
-    def prepare_queries(h):
-        for slot in range(4):
+    def prepare_queries(h, low):
+        def one(slot, c):
             sib_copy(h, slot).wait_recv()
-
-        def one(index, c):
-            half, place = index // 2, index % 2
+            half, place = slot_place(slot)
             for blk in range(2):
                 q1, q2, q3 = thirds(qb[h, half, place, blk, 0] * SCALE)
                 o1, o2 = halves(qb[h, half, place, blk, 1])
@@ -186,7 +194,7 @@
                     ro[h, half, rows, i * DIM:(i + 1) * DIM] = part
             return c
 
-        lax.fori_loop(0, 4, one, 0)
+        lax.fori_loop(low, low + 2, one, 0)
 
     def prepare_keys(h, line):
         for unit in range(3):
@@ -213,32 +221,43 @@
         st[index, 1:2] = jnp.sum(weights, axis=0, keepdims=True)
         st[index, 2:3] = jnp.sum(weights * dprobs, axis=0, keepdims=True)
 
-    def own_forward(h):
-        prepare_keys(h, 0)
-
-        def one(half, c):
-            forward_block(h, half, 0, half)
+    def forward(h, before):
+        def one(step, c):
+            for i in range(3):
+                @pl.when(step == i)
+                def _():
+                    before[i]()
+
+            half = jnp.where(step == 0, xl, 1 - xl)
+            line = step // 2
+            here = (step < 2) | y_in
+
+            @pl.when(here & (step != 1))
+            def _():
+                @pl.when(step == 2)
+                def _():
+                    for kv in range(2):
+                        y_copy(h, 0, kv).wait_recv()
+
+                        @pl.when(side_in)
+                        def _():
+                            y_copy(h, 1, kv).wait_recv()
+                            y_copy(h, 2, kv).wait_recv()
+
+                prepare_keys(h, line)
+
+            @pl.when(here)
+            def _():
+                forward_block(h, step, line, half)
+
+            @pl.when(jnp.logical_not(here))
+            def _():
+                st[3 * h + 2, 0:1] = jnp.full((1, HALF), LOW, F32)
+                st[3 * h + 2, 1:3] = jnp.zeros((2, HALF), F32)
+
             return c
 
-        lax.fori_loop(0, 2, one, 0)
-
-    def halo_forward(h):
-        @pl.when(y_in)
-        def _():
-            y_copy(h, 0).wait_recv()
-
-            @pl.when(side_in)
-            def _():
-                y_copy(h, 1).wait_recv()
-                y_copy(h, 2).wait_recv()
-
-            prepare_keys(h, 1)
-            forward_block(h, 2, 1, 1 - xl)
-
-        @pl.when(jnp.logical_not(y_in))
-        def _():
-            st[3 * h + 2, 0:1] = jnp.full((1, HALF), LOW, F32)
-            st[3 * h + 2, 1:3] = jnp.zeros((2, HALF), F32)
+        lax.fori_loop(0, 3, one, 0)
 
     me = 2 * xl + zp
 
@@ -265,15 +284,11 @@
         return remote(sall.at[h, me], sall.at[h, me], stat_sem, (h, which), device)
 
     def start_stats(h):
+        merged = (triple(st.at[3 * h], 0), merge([triple(st.at[3 * h + 1], 0), triple(st.at[3 * h + 2], 0)]))
         for half in range(2):
-            mine = half == 1 - xl
-            extra = triple(st.at[3 * h + 2], 0)
-            extra = (
-                jnp.where(mine, extra[0], LOW), jnp.where(mine, extra[1], 0.0), jnp.where(mine, extra[2], 0.0)
-            )
-            merged = merge([triple(st.at[3 * h + half], 0), extra])
             for i in range(3):
-                sst[h, core, 3 * half + i:3 * half + i + 1] = merged[i]
+                value = jnp.where(half == xl, merged[0][i], merged[1][i])
+                sst[h, core, 3 * half + i:3 * half + i + 1] = value
         sst[h, core, 6:8] = jnp.zeros((2, HALF), F32)
         pair_copy(h).start()
 
@@ -327,28 +342,36 @@
         dqt[h] = jnp.zeros(dqt.shape[1:], F32)
         own[h] = jnp.zeros(own.shape[1:], F32)
 
-        @pl.when(y_in)
-        def _():
-            dk, dv = backward_block(h, 2, 1, 1 - xl)
-            for unit in range(3):
-                halo[h, unit, 0] = dk[unit * CELLS:(unit + 1) * CELLS]
-                halo[h, unit, 1] = dv[unit * CELLS:(unit + 1) * CELLS]
-
-            @pl.when(side_in)
-            def _():
-                yr_copy(h, 2).start()
-                yr_copy(h, 1).start()
-
-            yr_copy(h, 0).start()
-
-        def one(half, c):
-            dk, dv = backward_block(h, half, 0, half)
-            for unit in range(3):
-                own[h, unit, 0] += dk[unit * CELLS:(unit + 1) * CELLS]
-                own[h, unit, 1] += dv[unit * CELLS:(unit + 1) * CELLS]
+        def one(turn, c):
+            step = 2 - turn
+
+            @pl.when((step < 2) | y_in)
+            def _():
+                half = jnp.where(step == 0, xl, 1 - xl)
+                dk, dv = backward_block(h, step, step // 2, half)
+
+                @pl.when(step == 2)
+                def _():
+                    for unit in range(3):
+                        halo[h, unit, 0] = dk[unit * CELLS:(unit + 1) * CELLS]
+                        halo[h, unit, 1] = dv[unit * CELLS:(unit + 1) * CELLS]
+
+                    @pl.when(side_in)
+                    def _():
+                        yr_copy(h, 2).start()
+                        yr_copy(h, 1).start()
+
+                    yr_copy(h, 0).start()
+
+                @pl.when(step < 2)
+                def _():
+                    for unit in range(3):
+                        own[h, unit, 0] += dk[unit * CELLS:(unit + 1) * CELLS]
+                        own[h, unit, 1] += dv[unit * CELLS:(unit + 1) * CELLS]
+
             return c
 
-        lax.fori_loop(0, 2, one, 0)
+        lax.fori_loop(0, 3, one, 0)
         dqs_copy(h).start()
 
     def dq_copy(h, which):
@@ -404,24 +427,28 @@
         dv_out[:, :, lanes] = own[h, 0, 1].reshape(32, 4, DIM)
 
     def all_left(h):
-        @pl.when(y_out)
-        def _():
-            y_copy(h, 0).wait_send()
+        for part in range(2):
+            @pl.when(y_out)
+            def _():
+                y_copy(h, 0, part).wait_send()
+
+                @pl.when(side_in)
+                def _():
+                    y_copy(h, 1, part).wait_send()
+                    y_copy(h, 2, part).wait_send()
 
             @pl.when(side_in)
             def _():
-                y_copy(h, 1).wait_send()
-                y_copy(h, 2).wait_send()
-
-        @pl.when(side_in)
-        def _():
-            near_copy(h).wait_send()
-            for which in range(2):
-                zr_copy(h, which).wait_send()
-
-        @pl.when(far_out)
-        def _():
-            far_copy(h).wait_send()
+                near_copy(h, part).wait_send()
+                zr_copy(h, part).wait_send()
+
+            @pl.when(far_out)
+            def _():
+                far_copy(h, part).wait_send()
+
+            zq_copy(h, part).wait_send()
+            xq_copy(h, part).wait_send()
+            diag_by_x(h, part).wait_send()
 
         @pl.when(y_in)
         def _():
@@ -432,9 +459,6 @@
                 yr_copy(h, 1).wait_send()
                 yr_copy(h, 2).wait_send()
 
-        zq_copy(h).wait_send()
-        xq_copy(h).wait_send()
-        diag_by_x(h).wait_send()
         for slot in range(4):
             sib_copy(h, slot).wait_send()
         pair_copy(h).wait_send()
@@ -444,6 +468,7 @@
             dq_copy(h, which).wait_send()
 
     first_sends(0)
+    first_sends(1)
 
     @pl.when(jnp.logical_not(side_in))
     def _():
@@ -451,21 +476,36 @@
             for line in range(2):
                 kvb[h, line, 1:3] = jnp.zeros((2, 2, CELLS, DIM), F32)
 
-    pass_on(0)
-    first_sends(1)
-    last_queries(0)
-    prepare_queries(0)
-    own_forward(0)
-    pass_on(1)
-    halo_forward(0)
+    def head0_start():
+        pass_keys(0, 0)
+        pass_keys(0, 1)
+        pass_queries(0)
+        prepare_queries(0, 0)
+
+    def head0_other():
+        last_queries(0)
+        prepare_queries(0, 2)
+
+    def head0_halo():
+        pass_keys(1, 0)
+
+    def head1_start():
+        prepare_queries(1, 0)
+
+    def head1_other():
+        last_queries(1)
+        prepare_queries(1, 2)
+
+    def head1_halo():
+        end_stats(0)
+        backward(0)
+
+    forward(0, (head0_start, head0_other, head0_halo))
     start_stats(0)
-    last_queries(1)
+    pass_keys(1, 1)
+    pass_queries(1)
     share_stats(0)
-    prepare_queries(1)
-    own_forward(1)
-    end_stats(0)
-    backward(0)
-    halo_forward(1)
+    forward(1, (head1_start, head1_other, head1_halo))
     start_stats(1)
     share_dq(0)
     share_stats(1)
@@ -478,6 +518,14 @@
     finish(1)
     all_left(0)
     all_left(1)
+
+
+def copy_kernel(*refs):
+    copies = [pltpu.make_async_copy(refs[i], refs[3 + i], refs[6].at[i]) for i in range(3)]
+    for copy in copies:
+        copy.start()
+    for copy in copies:
+        copy.wait()
 
 
 def body(query_field, key_field, value_field, output_grad):
@@ -514,13 +562,20 @@
             pltpu.VMEM((2, 3, 2, CELLS, DIM), F32),
             pltpu.VMEM((2, 2, 2, CELLS, DIM), F32),
             pltpu.SemaphoreType.DMA((4,)),
-            sems(), sems(), sems(3), sems(), sems(), sems(), sems(4), sems(), sems(3),
+            sems(2), sems(2), sems(3, 2), sems(2), sems(2), sems(2), sems(4), sems(), sems(3),
             sems(3), sems(2), sems(), sems(3),
         ],
         compiler_params=pltpu.CompilerParams(
             collective_id=0, has_side_effects=True, vmem_limit_bytes=56 * 1024 * 1024
         ),
     )(*(x.reshape(flat) for x in (query_field, key_field, value_field, output_grad)))
+    outs = pl.pallas_call(
+        copy_kernel,
+        out_shape=[jax.ShapeDtypeStruct(flat, F32)] * 3,
+        in_specs=[pl.BlockSpec(memory_space=pl.ANY)] * 3,
+        out_specs=[pl.BlockSpec(memory_space=pl.ANY)] * 3,
+        scratch_shapes=[pltpu.SemaphoreType.DMA((3,))],
+    )(*outs)
     return tuple(x.reshape(frames, rows, cols, channels) for x in outs)
 
 

time: 70.7 us -> 79.3 us (1.12)
  the two profiles are of different devices: /device:TPU:1 before, /device:TPU:72 now
where the time goes in v3:
time: 79.3 us; the launch traced here: 79.2 us
  Pallas kernels  78.5 us (99%)
    pallas_call x1, Pallas kernels, body(): pl.pallas_call(kernel, out_shape=[jax.ShapeDtypeStruct(flat, F32)] * 3, i...  65.5 us
    pallas_call x1, Pallas kernels, body(): pl.pallas_call(copy_kernel, out_shape=[jax.ShapeDtypeStruct(flat, F32)] *...  13 us

profile of v3, /device:TPU:72, one launch (start us, length us, event | category | flops | bytes accessed | tf_op | source)
XLA Modules:
  0.0 79.2 jit_solution(17690422133153648625)
XLA Ops:
  0.6 65.5 %shard_map.67 = (f32[32,4,256]{2,1,0:T(4,128)}, f32[32,4,256]{2,1,0:T(4,128)}, f32[32,4,256]{2,1,0:T(4,128)}) custom-call(f32[32,4,256]{2,1,0:T(4,128)} %bitcast.7, f32[32,4,256]{2,1,0:T(4,128)} %bitcast.8, f32[32,4,256]{2,1,0:T(4,128)} %bitcast.9, f32[32,4,256]{2,1,0:T(4,128)} %bitcast.10), custom_call_target="tpu_custom_call" | custom-call | tf_op jit(solution)/shard_map/pallas_call | solution.py:538
  66.1 13.0 %shard_map.68 = (f32[32,4,256]{2,1,0:T(4,128)}, f32[32,4,256]{2,1,0:T(4,128)}, f32[32,4,256]{2,1,0:T(4,128)}) custom-call(f32[32,4,256]{2,1,0:T(4,128)} %get-tuple-element.9.refs_0_, f32[32,4,256]{2,1,0:T(4,128)} %get-tuple-element.10.refs_1_, f32[32,4,256]{2,1,0:T(4,128)} %get-tuple-element.11.refs_2_), custom_call_target="tpu_custom_call" | custom-call | tf_op jit(solution)/shard_map/pallas_call | solution.py:572

commit v4 on v3

--- a/solution.py
+++ b/solution.py
@@ -34,8 +34,8 @@
 
 def kernel(
     q_in, k_in, v_in, g_in, dq_out, dk_out, dv_out,
-    raw, kvb, qb, kp, lv, rq, ro, wbuf, dbuf, st, sst, sall, gst, dqt, dqs, dqr, own, halo, yret, zret,
-    in_sem, near_sem, far_sem, y_sem, zq_sem, xq_sem, diag_sem, sibq_sem, pair_sem, stat_sem,
+    raw, kvb, qb, kp, lv, rq, ro, wbuf, dbuf, rel, st, sst, sall, gst, dqt, dqs, dqr, own, halo, yret, zret,
+    in_sem, near_sem, far_sem, y_sem, zq_sem, xq_sem, diag_sem, sibq_sem, rel_sem, pair_sem, stat_sem,
     yr_sem, zr_sem, dqs_sem, dq_sem,
 ):
     ha, wa = lax.axis_index("ha"), lax.axis_index("wa")
@@ -67,6 +67,23 @@
     partners = (sib_id, near_id, far_to, far_from, zpair, xpair, diag, y_to, y_from)
     for device in partners:
         pl.semaphore_signal(barrier, inc=1, device_id=device, device_id_type=MESH)
+
+    to_relay = (chip == 6) | (chip == 9)
+    relay = (chip == 14) | (chip == 1)
+    from_relay = (chip == 8) | (chip == 7)
+    turn = jnp.where((chip == 6) | (chip == 1), 1, -1)
+    jump = jnp.where((chip == 1) | (chip == 8), 1, -1)
+    cross_id = (ha, (wa + 16 * turn + 32) % 32)
+    jump_id = (ha, (wa + 12 * jump + 32) % 32)
+
+    @pl.when(to_relay | relay)
+    def _():
+        pl.semaphore_signal(barrier, inc=1, device_id=cross_id, device_id_type=MESH)
+
+    @pl.when(relay | from_relay)
+    def _():
+        pl.semaphore_signal(barrier, inc=1, device_id=jump_id, device_id_type=MESH)
+
     loads = [
         pltpu.make_async_copy(ref, raw.at[i], in_sem.at[i]) for i, ref in enumerate((k_in, v_in, q_in, g_in))
     ]
@@ -81,7 +98,8 @@
                 kvb[h, 0, 0, i] = part
             else:
                 qb[h, xl, zp, core, i - 2] = part
-    pl.semaphore_wait(barrier, len(partners))
+    extra = jnp.where(relay, 2, jnp.where(to_relay | from_relay, 1, 0))
+    pl.semaphore_wait(barrier, len(partners) + extra)
 
     def remote(src, dst, sems, index, device):
         return pltpu.make_async_remote_copy(
@@ -95,6 +113,12 @@
     def far_copy(h, kv):
         return remote(kvb.at[h, 0, 0, kv], kvb.at[h, 0, 2, kv], far_sem, (h, kv), far_to)
 
+    def relay_copy(h, kv):
+        return remote(kvb.at[h, 0, 0, kv], rel.at[h, kv], rel_sem, (h, kv), cross_id)
+
+    def jump_copy(h, kv):
+        return remote(rel.at[h, kv], kvb.at[h, 0, 2, kv], far_sem, (h, kv), jump_id)
+
     def y_copy(h, unit, kv):
         return remote(kvb.at[h, 0, unit, kv], kvb.at[h, 1, unit, kv], y_sem, (h, unit, kv), y_to)
 
@@ -133,7 +157,11 @@
             def _():
                 near_copy(h, part).start()
 
-            @pl.when(far_out)
+            @pl.when(to_relay)
+            def _():
+                relay_copy(h, part).start()
+
+            @pl.when(far_out & jnp.logical_not(to_relay))
             def _():
                 far_copy(h, part).start()
 
@@ -142,6 +170,11 @@
         sib_copy(h, 0).start()
 
     def pass_keys(h, kv):
+        @pl.when(relay)
+        def _():
+            relay_copy(h, kv).wait_recv()
+            jump_copy(h, kv).start()
+
         @pl.when(side_in)
         def _():
             near_copy(h, kv).wait_recv()
@@ -172,6 +205,8 @@
         def _():
             diag_by_z(h, 0).start()
 
+    def last_pass(h):
+        pass_keys(h, 1)
         zq_copy(h, 1).wait_recv()
         sib_copy(h, 1).start()
 
@@ -332,8 +367,8 @@
                 dqt[h, half, place, blk] += dq[:, at:at + CELLS]
         return dk[:, :DIM] + dk[:, DIM:], dv[:, :DIM] + dv[:, DIM:]
 
-    def yr_copy(h, unit):
-        return remote(halo.at[h, unit], yret.at[h, unit], yr_sem, (h, unit), y_from)
+    def yr_copy(h, unit, kind):
+        return remote(halo.at[h, unit, kind], yret.at[h, unit, kind], yr_sem, (h, unit, kind), y_from)
 
     def dqs_copy(h):
         return remote(dqt.at[h, :, :, 1 - core], dqs.at[h], dqs_sem, (h,), sib_id)
@@ -358,10 +393,12 @@
 
                     @pl.when(side_in)
                     def _():
-                        yr_copy(h, 2).start()
-                        yr_copy(h, 1).start()
-
-                    yr_copy(h, 0).start()
+                        for unit in (2, 1):
+                            for kind in range(2):
+                                yr_copy(h, unit, kind).start()
+
+                    for kind in range(2):
+                        yr_copy(h, 0, kind).start()
 
                 @pl.when(step < 2)
                 def _():
@@ -387,19 +424,21 @@
         for which in range(3):
             dq_copy(h, which).start()
 
-    def zr_copy(h, which):
-        return remote(own.at[h, 1 + which], zret.at[h, which], zr_sem, (h, which), (near_id, far_from)[which])
+    def zr_copy(h, which, kind):
+        device = (near_id, far_from)[which]
+        return remote(own.at[h, 1 + which, kind], zret.at[h, which, kind], zr_sem, (h, which, kind), device)
 
     def pass_back(h):
         for which in (1, 0):
-            @pl.when(side_in)
-            def _():
-                @pl.when(y_out)
+            for kind in range(2):
+                @pl.when(side_in)
                 def _():
-                    yr_copy(h, 1 + which).wait_recv()
-                    own[h, 1 + which] += yret[h, 1 + which]
-
-                zr_copy(h, which).start()
+                    @pl.when(y_out)
+                    def _():
+                        yr_copy(h, 1 + which, kind).wait_recv()
+                        own[h, 1 + which, kind] += yret[h, 1 + which, kind]
+
+                    zr_copy(h, which, kind).start()
 
     def finish(h):
         lanes = slice(h * DIM, (h + 1) * DIM)
@@ -410,17 +449,20 @@
 
         @pl.when(y_out)
         def _():
-            yr_copy(h, 0).wait_recv()
+            yr_copy(h, 0, 0).wait_recv()
+            yr_copy(h, 0, 1).wait_recv()
             own[h, 0] += yret[h, 0]
 
         @pl.when(far_out)
         def _():
-            zr_copy(h, 1).wait_recv()
+            zr_copy(h, 1, 0).wait_recv()
+            zr_copy(h, 1, 1).wait_recv()
             own[h, 0] += zret[h, 1]
 
         @pl.when(side_in)
         def _():
-            zr_copy(h, 0).wait_recv()
+            zr_copy(h, 0, 0).wait_recv()
+            zr_copy(h, 0, 1).wait_recv()
             own[h, 0] += zret[h, 0]
 
         dk_out[:, :, lanes] = own[h, 0, 0].reshape(32, 4, DIM)
@@ -440,9 +482,14 @@
             @pl.when(side_in)
             def _():
                 near_copy(h, part).wait_send()
-                zr_copy(h, part).wait_send()
-
-            @pl.when(far_out)
+                zr_copy(h, 0, part).wait_send()
+                zr_copy(h, 1, part).wait_send()
+
+            @pl.when(to_relay)
+            def _():
+                relay_copy(h, part).wait_send()
+
+            @pl.when((far_out & jnp.logical_not(to_relay)) | relay)
             def _():
                 far_copy(h, part).wait_send()
 
@@ -452,12 +499,13 @@
 
         @pl.when(y_in)
         def _():
-            yr_copy(h, 0).wait_send()
-
-            @pl.when(side_in)
-            def _():
-                yr_copy(h, 1).wait_send()
-                yr_copy(h, 2).wait_send()
+            for kind in range(2):
+                yr_copy(h, 0, kind).wait_send()
+
+                @pl.when(side_in)
+                def _():
+                    yr_copy(h, 1, kind).wait_send()
+                    yr_copy(h, 2, kind).wait_send()
 
         for slot in range(4):
             sib_copy(h, slot).wait_send()
@@ -478,8 +526,8 @@
 
     def head0_start():
         pass_keys(0, 0)
-        pass_keys(0, 1)
         pass_queries(0)
+        last_pass(0)
         prepare_queries(0, 0)
 
     def head0_other():
@@ -502,8 +550,8 @@
 
     forward(0, (head0_start, head0_other, head0_halo))
     start_stats(0)
-    pass_keys(1, 1)
     pass_queries(1)
+    last_pass(1)
     share_stats(0)
     forward(1, (head1_start, head1_other, head1_halo))
     start_stats(1)
@@ -512,8 +560,8 @@
     pass_back(0)
     end_stats(1)
     backward(1)
+    share_dq(1)
     finish(0)
-    share_dq(1)
     pass_back(1)
     finish(1)
     all_left(0)
@@ -521,11 +569,8 @@
 
 
 def copy_kernel(*refs):
-    copies = [pltpu.make_async_copy(refs[i], refs[3 + i], refs[6].at[i]) for i in range(3)]
-    for copy in copies:
-        copy.start()
-    for copy in copies:
-        copy.wait()
+    for i in range(3):
+        refs[3 + i][...] = refs[i][...]
 
 
 def body(query_field, key_field, value_field, output_grad):
@@ -550,6 +595,7 @@
             pltpu.VMEM((2, 2, HALF, 4 * DIM), BF16),
             pltpu.VMEM((6, KEYS, HALF), F32),
             pltpu.VMEM((6, KEYS, HALF), F32),
+            pltpu.VMEM((2, 2, CELLS, DIM), F32),
             pltpu.VMEM((6, 8, HALF), F32),
             pltpu.VMEM((2, 2, 8, HALF), F32),
             pltpu.VMEM((2, 4, 8, HALF), F32),
@@ -562,8 +608,8 @@
             pltpu.VMEM((2, 3, 2, CELLS, DIM), F32),
             pltpu.VMEM((2, 2, 2, CELLS, DIM), F32),
             pltpu.SemaphoreType.DMA((4,)),
-            sems(2), sems(2), sems(3, 2), sems(2), sems(2), sems(2), sems(4), sems(), sems(3),
-            sems(3), sems(2), sems(), sems(3),
+            sems(2), sems(2), sems(3, 2), sems(2), sems(2), sems(2), sems(4), sems(2), sems(), sems(3),
+            sems(3, 2), sems(2, 2), sems(), sems(3),
         ],
         compiler_params=pltpu.CompilerParams(
             collective_id=0, has_side_effects=True, vmem_limit_bytes=56 * 1024 * 1024
@@ -572,9 +618,8 @@
     outs = pl.pallas_call(
         copy_kernel,
         out_shape=[jax.ShapeDtypeStruct(flat, F32)] * 3,
-        in_specs=[pl.BlockSpec(memory_space=pl.ANY)] * 3,
-        out_specs=[pl.BlockSpec(memory_space=pl.ANY)] * 3,
-        scratch_shapes=[pltpu.SemaphoreType.DMA((3,))],
+        in_specs=[pl.BlockSpec(memory_space=pltpu.VMEM)] * 3,
+        out_specs=[pl.BlockSpec(memory_space=pltpu.VMEM)] * 3,
     )(*outs)
     return tuple(x.reshape(frames, rows, cols, channels) for x in outs)
 

time: 79.3 us -> 66.9 us (0.84)
  the two profiles are of different devices: /device:TPU:72 before, /device:TPU:14 now
where the time goes in v4:
time: 66.9 us; the launch traced here: 66.7 us
  Pallas kernels  66.1 us (99%)
    pallas_call x1, Pallas kernels, body(): pl.pallas_call(kernel, out_shape=[jax.ShapeDtypeStruct(flat, F32)] * 3, i...  64.3 us
    pallas_call x1, Pallas kernels, body(): pl.pallas_call(copy_kernel, out_shape=[jax.ShapeDtypeStruct(flat, F32)] *...  1.78 us

profile of v4, /device:TPU:14, one launch (start us, length us, event | category | flops | bytes accessed | tf_op | source)
XLA Modules:
  0.0 66.7 jit_solution(4670750282979417468)
XLA Ops:
  0.6 64.3 %shard_map.67 = (f32[32,4,256]{2,1,0:T(4,128)}, f32[32,4,256]{2,1,0:T(4,128)}, f32[32,4,256]{2,1,0:T(4,128)}) custom-call(f32[32,4,256]{2,1,0:T(4,128)} %bitcast.7, f32[32,4,256]{2,1,0:T(4,128)} %bitcast.8, f32[32,4,256]{2,1,0:T(4,128)} %bitcast.9, f32[32,4,256]{2,1,0:T(4,128)} %bitcast.10), custom_call_target="tpu_custom_call" | custom-call | tf_op jit(solution)/shard_map/pallas_call | solution.py:583
  65.0 1.8 %shard_map.68 = (f32[32,4,256]{2,1,0:T(4,128)}, f32[32,4,256]{2,1,0:T(4,128)}, f32[32,4,256]{2,1,0:T(4,128)}) custom-call(f32[32,4,256]{2,1,0:T(4,128)} %get-tuple-element.9.refs_0_, f32[32,4,256]{2,1,0:T(4,128)} %get-tuple-element.10.refs_1_, f32[32,4,256]{2,1,0:T(4,128)} %get-tuple-element.11.refs_2_), custom_call_target="tpu_custom_call" | custom-call | tf_op jit(solution)/shard_map/pallas_call | solution.py:618

commit v5 on v4

--- a/solution.py
+++ b/solution.py
@@ -34,8 +34,8 @@
 
 def kernel(
     q_in, k_in, v_in, g_in, dq_out, dk_out, dv_out,
-    raw, kvb, qb, kp, lv, rq, ro, wbuf, dbuf, rel, st, sst, sall, gst, dqt, dqs, dqr, own, halo, yret, zret,
-    in_sem, near_sem, far_sem, y_sem, zq_sem, xq_sem, diag_sem, sibq_sem, rel_sem, pair_sem, stat_sem,
+    raw, kvb, qb, kp, lv, rq, ro, wbuf, dbuf, rel, st, sall, gst, dqt, dqs, dqr, own, halo, yret, zret,
+    in_sem, near_sem, far_sem, y_sem, zq_sem, xq_sem, diag_sem, sibq_sem, rel_sem, stat_sem,
     yr_sem, zr_sem, dqs_sem, dq_sem,
 ):
     ha, wa = lax.axis_index("ha"), lax.axis_index("wa")
@@ -64,7 +64,9 @@
     z_first = (tile > 0) & (tile < 7)
 
     barrier = pltpu.get_barrier_semaphore()
-    partners = (sib_id, near_id, far_to, far_from, zpair, xpair, diag, y_to, y_from)
+    flip = 1 - 2 * core
+    group = (diag, zpair, xpair, (ha - up, wa - 2 * side + flip), (ha, wa - 2 * side + flip), (ha - up, wa + flip), sib_id)
+    partners = group + (near_id, far_to, far_from, y_to, y_from)
     for device in partners:
         pl.semaphore_signal(barrier, inc=1, device_id=device, device_id_type=MESH)
 
@@ -146,12 +148,18 @@
         block = qb.at[h, half, place, core]
         return remote(block, block, sibq_sem, (h, slot), sib_id)
 
-    def first_sends(h):
+    def y_sends(h):
         @pl.when(y_out)
         def _():
             y_copy(h, 0, 0).start()
             y_copy(h, 0, 1).start()
 
+    def x_sends(h):
+        for part in (1, 0):
+            xq_copy(h, part).start()
+        sib_copy(h, 0).start()
+
+    def z_sends(h):
         for part in range(2):
             @pl.when(side_in)
             def _():
@@ -166,8 +174,6 @@
                 far_copy(h, part).start()
 
             zq_copy(h, part).start()
-            xq_copy(h, part).start()
-        sib_copy(h, 0).start()
 
     def pass_keys(h, kv):
         @pl.when(relay)
@@ -294,7 +300,7 @@
 
         lax.fori_loop(0, 3, one, 0)
 
-    me = 2 * xl + zp
+    me = 4 * xl + 2 * zp + core
 
     def merge(triples):
         peak = triples[0][0]
@@ -311,61 +317,50 @@
     def triple(ref, base):
         return tuple(ref[base + i:base + i + 1] for i in range(3))
 
-    def pair_copy(h):
-        return remote(sst.at[h, core], sst.at[h, core], pair_sem, (h,), sib_id)
-
     def stat_copy(h, which):
-        device = (xpair, zpair, diag)[which]
-        return remote(sall.at[h, me], sall.at[h, me], stat_sem, (h, which), device)
+        place = sall.at[h, me]
+        return remote(place, place, stat_sem, (h, which), group[which])
 
     def start_stats(h):
         merged = (triple(st.at[3 * h], 0), merge([triple(st.at[3 * h + 1], 0), triple(st.at[3 * h + 2], 0)]))
         for half in range(2):
             for i in range(3):
                 value = jnp.where(half == xl, merged[0][i], merged[1][i])
-                sst[h, core, 3 * half + i:3 * half + i + 1] = value
-        sst[h, core, 6:8] = jnp.zeros((2, HALF), F32)
-        pair_copy(h).start()
-
-    def share_stats(h):
-        pair_copy(h).wait_recv()
-        for half in range(2):
-            merged = merge([triple(sst.at[h, i], 3 * half) for i in range(2)])
-            for i in range(3):
-                sall[h, me, 3 * half + i:3 * half + i + 1] = merged[i]
+                sall[h, me, 3 * half + i:3 * half + i + 1] = value
         sall[h, me, 6:8] = jnp.zeros((2, HALF), F32)
-        for which in range(3):
+        for which in range(7):
             stat_copy(h, which).start()
 
     def end_stats(h):
-        for which in range(3):
+        for which in range(7):
             stat_copy(h, which).wait_recv()
         for half in range(2):
-            peak, total, center = merge([triple(sall.at[h, i], 3 * half) for i in range(4)])
+            peak, total, center = merge([triple(sall.at[h, i], 3 * half) for i in range(8)])
             inverse = 1.0 / total
             gst[h, half, 0:1] = peak
             gst[h, half, 1:2] = inverse
             gst[h, half, 2:3] = center * inverse
 
-    def backward_block(h, k, line, half):
+    def backward_block(h, k, line, half, give):
         index = 3 * h + k
         alpha = jnp.exp(st[index, 0:1] - gst[h, half, 0:1]) * gst[h, half, 1:2]
         probs = wbuf[index] * alpha
         dscores = probs * (dbuf[index] - gst[h, half, 2:3])
         p1, p2 = halves(probs)
+        o12 = ro[h, half, :, DIM:3 * DIM]
+        dv = dot(p1, o12, ((1,), (0,))) + dot(p2, o12, ((1,), (0,)))
+        give(1, dv[:, :DIM] + dv[:, DIM:])
         s1, s2 = halves(dscores)
         q12 = rq[h, half, :, DIM:3 * DIM]
-        o12 = ro[h, half, :, DIM:3 * DIM]
+        dk = dot(s1, q12, ((1,), (0,))) + dot(s2, q12, ((1,), (0,)))
+        give(0, dk[:, :DIM] + dk[:, DIM:])
         k12 = kp[2 * h + line, :, 0:2 * DIM]
-        dv = dot(p1, o12, ((1,), (0,))) + dot(p2, o12, ((1,), (0,)))
-        dk = dot(s1, q12, ((1,), (0,))) + dot(s2, q12, ((1,), (0,)))
         dq = dot(k12, s1, ((0,), (0,))) + dot(k12, s2, ((0,), (0,)))
         dq = dq[:DIM] + dq[DIM:]
         for place in range(2):
             for blk in range(2):
                 at = (2 * place + blk) * CELLS
                 dqt[h, half, place, blk] += dq[:, at:at + CELLS]
-        return dk[:, :DIM] + dk[:, DIM:], dv[:, :DIM] + dv[:, DIM:]
 
     def yr_copy(h, unit, kind):
         return remote(halo.at[h, unit, kind], yret.at[h, unit, kind], yr_sem, (h, unit, kind), y_from)
@@ -383,28 +378,28 @@
             @pl.when((step < 2) | y_in)
             def _():
                 half = jnp.where(step == 0, xl, 1 - xl)
-                dk, dv = backward_block(h, step, step // 2, half)
-
-                @pl.when(step == 2)
-                def _():
-                    for unit in range(3):
-                        halo[h, unit, 0] = dk[unit * CELLS:(unit + 1) * CELLS]
-                        halo[h, unit, 1] = dv[unit * CELLS:(unit + 1) * CELLS]
-
-                    @pl.when(side_in)
+
+                def give(kind, value):
+                    @pl.when(step == 2)
                     def _():
-                        for unit in (2, 1):
-                            for kind in range(2):
-                                yr_copy(h, unit, kind).start()
-
-                    for kind in range(2):
-                        yr_copy(h, 0, kind).start()
-
-                @pl.when(step < 2)
-                def _():
-                    for unit in range(3):
-                        own[h, unit, 0] += dk[unit * CELLS:(unit + 1) * CELLS]
-                        own[h, unit, 1] += dv[unit * CELLS:(unit + 1) * CELLS]
+                        for unit in range(3):
+                            halo[h, unit, kind] = value[unit * CELLS:(unit + 1) * CELLS]
+
+                        @pl.when(side_in)
+                        def _():
+                            yr_copy(h, 2, kind).start()
+                            yr_copy(h, 1, kind).start()
+
+                        if kind == 0:
+                            yr_copy(h, 0, 0).start()
+                            yr_copy(h, 0, 1).start()
+
+                    @pl.when(step < 2)
+                    def _():
+                        for unit in range(3):
+                            own[h, unit, kind] += value[unit * CELLS:(unit + 1) * CELLS]
+
+                backward_block(h, step, step // 2, half, give)
 
             return c
 
@@ -429,8 +424,8 @@
         return remote(own.at[h, 1 + which, kind], zret.at[h, which, kind], zr_sem, (h, which, kind), device)
 
     def pass_back(h):
-        for which in (1, 0):
-            for kind in range(2):
+        for kind in (1, 0):
+            for which in (1, 0):
                 @pl.when(side_in)
                 def _():
                     @pl.when(y_out)
@@ -509,14 +504,15 @@
 
         for slot in range(4):
             sib_copy(h, slot).wait_send()
-        pair_copy(h).wait_send()
         dqs_copy(h).wait_send()
         for which in range(3):
+            dq_copy(h, which).wait_send()
+        for which in range(7):
             stat_copy(h, which).wait_send()
-            dq_copy(h, which).wait_send()
-
-    first_sends(0)
-    first_sends(1)
+
+    y_sends(0)
+    z_sends(0)
+    x_sends(0)
 
     @pl.when(jnp.logical_not(side_in))
     def _():
@@ -527,7 +523,10 @@
     def head0_start():
         pass_keys(0, 0)
         pass_queries(0)
+        z_sends(1)
+        x_sends(1)
         last_pass(0)
+        y_sends(1)
         prepare_queries(0, 0)
 
     def head0_other():
@@ -541,22 +540,20 @@
         prepare_queries(1, 0)
 
     def head1_other():
+        end_stats(0)
+        backward(0)
         last_queries(1)
         prepare_queries(1, 2)
 
     def head1_halo():
-        end_stats(0)
-        backward(0)
+        share_dq(0)
 
     forward(0, (head0_start, head0_other, head0_halo))
     start_stats(0)
     pass_queries(1)
     last_pass(1)
-    share_stats(0)
     forward(1, (head1_start, head1_other, head1_halo))
     start_stats(1)
-    share_dq(0)
-    share_stats(1)
     pass_back(0)
     end_stats(1)
     backward(1)
@@ -597,8 +594,7 @@
             pltpu.VMEM((6, KEYS, HALF), F32),
             pltpu.VMEM((2, 2, CELLS, DIM), F32),
             pltpu.VMEM((6, 8, HALF), F32),
-            pltpu.VMEM((2, 2, 8, HALF), F32),
-            pltpu.VMEM((2, 4, 8, HALF), F32),
+            pltpu.VMEM((2, 8, 8, HALF), F32),
             pltpu.VMEM((2, 2, 8, HALF), F32),
             pltpu.VMEM((2, 2, 2, 2, DIM, CELLS), F32),
             pltpu.VMEM((2, 2, 2, DIM, CELLS), F32),
@@ -608,7 +604,7 @@
             pltpu.VMEM((2, 3, 2, CELLS, DIM), F32),
             pltpu.VMEM((2, 2, 2, CELLS, DIM), F32),
             pltpu.SemaphoreType.DMA((4,)),
-            sems(2), sems(2), sems(3, 2), sems(2), sems(2), sems(2), sems(4), sems(2), sems(), sems(3),
+            sems(2), sems(2), sems(3, 2), sems(2), sems(2), sems(2), sems(4), sems(2), sems(7),
             sems(3, 2), sems(2, 2), sems(), sems(3),
         ],
         compiler_params=pltpu.CompilerParams(

time: 66.9 us -> 67.2 us (level)
  no operation moved by 1% of the time
where the time goes in v5:
time: 67.2 us; the launch traced here: 66.9 us
  Pallas kernels  66.3 us (99%)
    pallas_call x1, Pallas kernels, body(): pl.pallas_call(kernel, out_shape=[jax.ShapeDtypeStruct(flat, F32)] * 3, i...  64.5 us
    pallas_call x1, Pallas kernels, body(): pl.pallas_call(copy_kernel, out_shape=[jax.ShapeDtypeStruct(flat, F32)] *...  1.78 us

profile of v5, /device:TPU:14, one launch (start us, length us, event | category | flops | bytes accessed | tf_op | source)
XLA Modules:
  0.0 66.9 jit_solution(6585817247311186026)
XLA Ops:
  0.6 64.5 %shard_map.67 = (f32[32,4,256]{2,1,0:T(4,128)}, f32[32,4,256]{2,1,0:T(4,128)}, f32[32,4,256]{2,1,0:T(4,128)}) custom-call(f32[32,4,256]{2,1,0:T(4,128)} %bitcast.7, f32[32,4,256]{2,1,0:T(4,128)} %bitcast.8, f32[32,4,256]{2,1,0:T(4,128)} %bitcast.9, f32[32,4,256]{2,1,0:T(4,128)} %bitcast.10), custom_call_target="tpu_custom_call" | custom-call | tf_op jit(solution)/shard_map/pallas_call | solution.py:580
  65.2 1.8 %shard_map.68 = (f32[32,4,256]{2,1,0:T(4,128)}, f32[32,4,256]{2,1,0:T(4,128)}, f32[32,4,256]{2,1,0:T(4,128)}) custom-call(f32[32,4,256]{2,1,0:T(4,128)} %get-tuple-element.9.refs_0_, f32[32,4,256]{2,1,0:T(4,128)} %get-tuple-element.10.refs_1_, f32[32,4,256]{2,1,0:T(4,128)} %get-tuple-element.11.refs_2_), custom_call_target="tpu_custom_call" | custom-call | tf_op jit(solution)/shard_map/pallas_call | solution.py:614

commit v6 on v5

--- a/solution.py
+++ b/solution.py
@@ -91,15 +91,18 @@
     ]
     for load in loads:
         load.start()
-    for load in loads:
-        load.wait()
-    for h in range(2):
-        for i in range(4):
+
+    def arrange(h, arrays):
+        for i in arrays:
             part = raw[i, :, :, h * DIM:(h + 1) * DIM].reshape(CELLS, DIM)
             if i < 2:
                 kvb[h, 0, 0, i] = part
             else:
                 qb[h, xl, zp, core, i - 2] = part
+
+    for load in loads:
+        load.wait()
+    arrange(0, range(4))
     extra = jnp.where(relay, 2, jnp.where(to_relay | from_relay, 1, 0))
     pl.semaphore_wait(barrier, len(partners) + extra)
 
@@ -347,20 +350,20 @@
         probs = wbuf[index] * alpha
         dscores = probs * (dbuf[index] - gst[h, half, 2:3])
         p1, p2 = halves(probs)
+        s1, s2 = halves(dscores)
         o12 = ro[h, half, :, DIM:3 * DIM]
+        q12 = rq[h, half, :, DIM:3 * DIM]
+        k12 = kp[2 * h + line, :, 0:2 * DIM].T
         dv = dot(p1, o12, ((1,), (0,))) + dot(p2, o12, ((1,), (0,)))
-        give(1, dv[:, :DIM] + dv[:, DIM:])
-        s1, s2 = halves(dscores)
-        q12 = rq[h, half, :, DIM:3 * DIM]
         dk = dot(s1, q12, ((1,), (0,))) + dot(s2, q12, ((1,), (0,)))
-        give(0, dk[:, :DIM] + dk[:, DIM:])
-        k12 = kp[2 * h + line, :, 0:2 * DIM]
-        dq = dot(k12, s1, ((0,), (0,))) + dot(k12, s2, ((0,), (0,)))
+        dq = dot(jnp.concatenate([k12, k12], axis=1), jnp.concatenate([s1, s2], axis=0), ((1,), (0,)))
         dq = dq[:DIM] + dq[DIM:]
         for place in range(2):
             for blk in range(2):
                 at = (2 * place + blk) * CELLS
                 dqt[h, half, place, blk] += dq[:, at:at + CELLS]
+        give(1, dv[:, :DIM] + dv[:, DIM:])
+        give(0, dk[:, :DIM] + dk[:, DIM:])
 
     def yr_copy(h, unit, kind):
         return remote(halo.at[h, unit, kind], yret.at[h, unit, kind], yr_sem, (h, unit, kind), y_from)
@@ -513,6 +516,7 @@
     y_sends(0)
     z_sends(0)
     x_sends(0)
+    arrange(1, range(4))
 
     @pl.when(jnp.logical_not(side_in))
     def _():

time: 67.2 us -> 63.6 us (0.946)
  Pallas kernels: 66.3 us -> 62.9 us
    pallas_call x1, Pallas kernels: 64.5 us -> 61.1 us  [body(): pl.pallas_call(kernel, out_shape=[jax.ShapeDtypeStruct(flat, F32)] * 3, i...]
where the time goes in v6:
time: 63.6 us; the launch traced here: 63.5 us
  Pallas kernels  62.9 us (99%)
  between operations  0.64 us (1%)
    pallas_call x1, Pallas kernels, body(): pl.pallas_call(kernel, out_shape=[jax.ShapeDtypeStruct(flat, F32)] * 3, i...  61.1 us
    pallas_call x1, Pallas kernels, body(): pl.pallas_call(copy_kernel, out_shape=[jax.ShapeDtypeStruct(flat, F32)] *...  1.78 us

profile of v6, /device:TPU:14, one launch (start us, length us, event | category | flops | bytes accessed | tf_op | source)
XLA Modules:
  0.0 63.5 jit_solution(5573421863234066195)
XLA Ops:
  0.6 61.1 %shard_map.67 = (f32[32,4,256]{2,1,0:T(4,128)}, f32[32,4,256]{2,1,0:T(4,128)}, f32[32,4,256]{2,1,0:T(4,128)}) custom-call(f32[32,4,256]{2,1,0:T(4,128)} %bitcast.7, f32[32,4,256]{2,1,0:T(4,128)} %bitcast.8, f32[32,4,256]{2,1,0:T(4,128)} %bitcast.9, f32[32,4,256]{2,1,0:T(4,128)} %bitcast.10), custom_call_target="tpu_custom_call" | custom-call | tf_op jit(solution)/shard_map/pallas_call | solution.py:584
  61.7 1.8 %shard_map.68 = (f32[32,4,256]{2,1,0:T(4,128)}, f32[32,4,256]{2,1,0:T(4,128)}, f32[32,4,256]{2,1,0:T(4,128)}) custom-call(f32[32,4,256]{2,1,0:T(4,128)} %get-tuple-element.9.refs_0_, f32[32,4,256]{2,1,0:T(4,128)} %get-tuple-element.10.refs_1_, f32[32,4,256]{2,1,0:T(4,128)} %get-tuple-element.11.refs_2_), custom_call_target="tpu_custom_call" | custom-call | tf_op jit(solution)/shard_map/pallas_call | solution.py:618

commit v7 on v6

--- a/solution.py
+++ b/solution.py
@@ -61,7 +61,6 @@
     far_out = jnp.where(zp == 0, tile < 7, tile > 0)
     y_out = jnp.where(xl == 1, row < 3, row > 0)
     y_in = jnp.where(xl == 1, row > 0, row < 3)
-    z_first = (tile > 0) & (tile < 7)
 
     barrier = pltpu.get_barrier_semaphore()
     flip = 1 - 2 * core
@@ -137,9 +136,6 @@
     def xq_copy(h, part):
         return q_copy(h, xl, zp, part, xq_sem, xpair)
 
-    def diag_by_x(h, part):
-        return q_copy(h, xl, 1 - zp, part, diag_sem, xpair)
-
     def diag_by_z(h, part):
         return q_copy(h, 1 - xl, zp, part, diag_sem, zpair)
 
@@ -202,17 +198,9 @@
         xq_copy(h, 1).wait_recv()
         diag_by_z(h, 1).start()
         zq_copy(h, 0).wait_recv()
-
-        @pl.when(z_first)
-        def _():
-            diag_by_x(h, 0).start()
-
         xq_copy(h, 0).wait_recv()
         sib_copy(h, 2).start()
-
-        @pl.when(jnp.logical_not(z_first))
-        def _():
-            diag_by_z(h, 0).start()
+        diag_by_z(h, 0).start()
 
     def last_pass(h):
         pass_keys(h, 1)
@@ -221,7 +209,7 @@
 
     def last_queries(h):
         for part in range(2):
-            diag_by_x(h, part).wait_recv()
+            diag_by_z(h, part).wait_recv()
         sib_copy(h, 3).start()
 
     def prepare_queries(h, low):
@@ -493,7 +481,7 @@
 
             zq_copy(h, part).wait_send()
             xq_copy(h, part).wait_send()
-            diag_by_x(h, part).wait_send()
+            diag_by_z(h, part).wait_send()
 
         @pl.when(y_in)
         def _():
@@ -527,13 +515,13 @@
     def head0_start():
         pass_keys(0, 0)
         pass_queries(0)
+        last_pass(0)
         z_sends(1)
+        prepare_queries(0, 0)
+
+    def head0_other():
+        y_sends(1)
         x_sends(1)
-        last_pass(0)
-        y_sends(1)
-        prepare_queries(0, 0)
-
-    def head0_other():
         last_queries(0)
         prepare_queries(0, 2)
 
@@ -547,10 +535,11 @@
         end_stats(0)
         backward(0)
         last_queries(1)
+        share_dq(0)
         prepare_queries(1, 2)
 
     def head1_halo():
-        share_dq(0)
+        pass
 
     forward(0, (head0_start, head0_other, head0_halo))
     start_stats(0)

time: 63.6 us -> 62.4 us (0.981)
  Pallas kernels: 62.9 us -> 61.5 us
    pallas_call x1, Pallas kernels: 61.1 us -> 59.7 us  [body(): pl.pallas_call(kernel, out_shape=[jax.ShapeDtypeStruct(flat, F32)] * 3, i...]
where the time goes in v7:
time: 62.4 us; the launch traced here: 62.2 us
  Pallas kernels  61.5 us (99%)
  between operations  0.64 us (1%)
    pallas_call x1, Pallas kernels, body(): pl.pallas_call(kernel, out_shape=[jax.ShapeDtypeStruct(flat, F32)] * 3, i...  59.7 us
    pallas_call x1, Pallas kernels, body(): pl.pallas_call(copy_kernel, out_shape=[jax.ShapeDtypeStruct(flat, F32)] *...  1.78 us

profile of v7, /device:TPU:14, one launch (start us, length us, event | category | flops | bytes accessed | tf_op | source)
XLA Modules:
  0.0 62.2 jit_solution(16577624933658830697)
XLA Ops:
  0.6 59.7 %shard_map.67 = (f32[32,4,256]{2,1,0:T(4,128)}, f32[32,4,256]{2,1,0:T(4,128)}, f32[32,4,256]{2,1,0:T(4,128)}) custom-call(f32[32,4,256]{2,1,0:T(4,128)} %bitcast.7, f32[32,4,256]{2,1,0:T(4,128)} %bitcast.8, f32[32,4,256]{2,1,0:T(4,128)} %bitcast.9, f32[32,4,256]{2,1,0:T(4,128)} %bitcast.10), custom_call_target="tpu_custom_call" | custom-call | tf_op jit(solution)/shard_map/pallas_call | solution.py:573
  60.4 1.8 %shard_map.68 = (f32[32,4,256]{2,1,0:T(4,128)}, f32[32,4,256]{2,1,0:T(4,128)}, f32[32,4,256]{2,1,0:T(4,128)}) custom-call(f32[32,4,256]{2,1,0:T(4,128)} %get-tuple-element.9.refs_0_, f32[32,4,256]{2,1,0:T(4,128)} %get-tuple-element.10.refs_1_, f32[32,4,256]{2,1,0:T(4,128)} %get-tuple-element.11.refs_2_), custom_call_target="tpu_custom_call" | custom-call | tf_op jit(solution)/shard_map/pallas_call | solution.py:607

commit v8 on v7

--- a/solution.py
+++ b/solution.py
@@ -69,20 +69,18 @@
     for device in partners:
         pl.semaphore_signal(barrier, inc=1, device_id=device, device_id_type=MESH)
 
+    place8 = chip % 8
+    crossing = (place8 < 2) | (place8 > 5)
     to_relay = (chip == 6) | (chip == 9)
     relay = (chip == 14) | (chip == 1)
-    from_relay = (chip == 8) | (chip == 7)
-    turn = jnp.where((chip == 6) | (chip == 1), 1, -1)
-    jump = jnp.where((chip == 1) | (chip == 8), 1, -1)
-    cross_id = (ha, (wa + 16 * turn + 32) % 32)
-    jump_id = (ha, (wa + 12 * jump + 32) % 32)
-
-    @pl.when(to_relay | relay)
+    back_to = (chip == 8) | (chip == 7)
+    back_relay = (chip == 0) | (chip == 15)
+    cross_id = (ha, (wa + 16) % 32)
+    jump_id = (ha, (wa + 12 * jnp.where(place8 < 4, 1, -1) + 32) % 32)
+
+    @pl.when(crossing)
     def _():
         pl.semaphore_signal(barrier, inc=1, device_id=cross_id, device_id_type=MESH)
-
-    @pl.when(relay | from_relay)
-    def _():
         pl.semaphore_signal(barrier, inc=1, device_id=jump_id, device_id_type=MESH)
 
     loads = [
@@ -102,7 +100,7 @@
     for load in loads:
         load.wait()
     arrange(0, range(4))
-    extra = jnp.where(relay, 2, jnp.where(to_relay | from_relay, 1, 0))
+    extra = jnp.where(crossing, 2, 0)
     pl.semaphore_wait(barrier, len(partners) + extra)
 
     def remote(src, dst, sems, index, device):
@@ -414,6 +412,19 @@
         device = (near_id, far_from)[which]
         return remote(own.at[h, 1 + which, kind], zret.at[h, which, kind], zr_sem, (h, which, kind), device)
 
+    def back_copy(h, kind):
+        return remote(own.at[h, 2, kind], rel.at[h, kind], rel_sem, (h, kind), cross_id)
+
+    def back_jump(h, kind):
+        return remote(rel.at[h, kind], zret.at[h, 1, kind], zr_sem, (h, 1, kind), jump_id)
+
+    def relay_back(h):
+        @pl.when(back_relay)
+        def _():
+            for kind in (1, 0):
+                back_copy(h, kind).wait_recv()
+                back_jump(h, kind).start()
+
     def pass_back(h):
         for kind in (1, 0):
             for which in (1, 0):
@@ -424,7 +435,16 @@
                         yr_copy(h, 1 + which, kind).wait_recv()
                         own[h, 1 + which, kind] += yret[h, 1 + which, kind]
 
-                    zr_copy(h, which, kind).start()
+                    if which == 0:
+                        zr_copy(h, 0, kind).start()
+                    else:
+                        @pl.when(back_to)
+                        def _():
+                            back_copy(h, kind).start()
+
+                        @pl.when(jnp.logical_not(back_to))
+                        def _():
+                            zr_copy(h, 1, kind).start()
 
     def finish(h):
         lanes = slice(h * DIM, (h + 1) * DIM)
@@ -469,9 +489,12 @@
             def _():
                 near_copy(h, part).wait_send()
                 zr_copy(h, 0, part).wait_send()
+
+            @pl.when((side_in & jnp.logical_not(back_to)) | back_relay)
+            def _():
                 zr_copy(h, 1, part).wait_send()
 
-            @pl.when(to_relay)
+            @pl.when(to_relay | back_to)
             def _():
                 relay_copy(h, part).wait_send()
 
@@ -550,9 +573,11 @@
     pass_back(0)
     end_stats(1)
     backward(1)
+    relay_back(0)
     share_dq(1)
     finish(0)
     pass_back(1)
+    relay_back(1)
     finish(1)
     all_left(0)
     all_left(1)

time: 62.4 us -> 63.9 us (1.024)
  the two profiles are of different devices: /device:TPU:14 before, /device:TPU:46 now
where the time goes in v8:
time: 63.9 us; the launch traced here: 63.8 us
  Pallas kernels  63.1 us (99%)
  between operations  0.64 us (1%)
    pallas_call x1, Pallas kernels, body(): pl.pallas_call(kernel, out_shape=[jax.ShapeDtypeStruct(flat, F32)] * 3, i...  61.4 us
    pallas_call x1, Pallas kernels, body(): pl.pallas_call(copy_kernel, out_shape=[jax.ShapeDtypeStruct(flat, F32)] *...  1.78 us

profile of v8, /device:TPU:46, one launch (start us, length us, event | category | flops | bytes accessed | tf_op | source)
XLA Modules:
  0.0 63.8 jit_solution(1171593017278247638)
XLA Ops:
  0.6 61.4 %shard_map.67 = (f32[32,4,256]{2,1,0:T(4,128)}, f32[32,4,256]{2,1,0:T(4,128)}, f32[32,4,256]{2,1,0:T(4,128)}) custom-call(f32[32,4,256]{2,1,0:T(4,128)} %bitcast.7, f32[32,4,256]{2,1,0:T(4,128)} %bitcast.8, f32[32,4,256]{2,1,0:T(4,128)} %bitcast.9, f32[32,4,256]{2,1,0:T(4,128)} %bitcast.10), custom_call_target="tpu_custom_call" | custom-call | tf_op jit(solution)/shard_map/pallas_call | solution.py:598
  62.0 1.8 %shard_map.68 = (f32[32,4,256]{2,1,0:T(4,128)}, f32[32,4,256]{2,1,0:T(4,128)}, f32[32,4,256]{2,1,0:T(4,128)}) custom-call(f32[32,4,256]{2,1,0:T(4,128)} %get-tuple-element.9.refs_0_, f32[32,4,256]{2,1,0:T(4,128)} %get-tuple-element.10.refs_1_, f32[32,4,256]{2,1,0:T(4,128)} %get-tuple-element.11.refs_2_), custom_call_target="tpu_custom_call" | custom-call | tf_op jit(solution)/shard_map/pallas_call | solution.py:632

commit v9 on v7

--- a/solution.py
+++ b/solution.py
@@ -360,9 +360,6 @@
         return remote(dqt.at[h, :, :, 1 - core], dqs.at[h], dqs_sem, (h,), sib_id)
 
     def backward(h):
-        dqt[h] = jnp.zeros(dqt.shape[1:], F32)
-        own[h] = jnp.zeros(own.shape[1:], F32)
-
         def one(turn, c):
             step = 2 - turn
 
@@ -505,6 +502,8 @@
     z_sends(0)
     x_sends(0)
     arrange(1, range(4))
+    dqt[...] = jnp.zeros(dqt.shape, F32)
+    own[...] = jnp.zeros(own.shape, F32)
 
     @pl.when(jnp.logical_not(side_in))
     def _():
@@ -559,8 +558,21 @@
 
 
 def copy_kernel(*refs):
-    for i in range(3):
-        refs[3 + i][...] = refs[i][...]
+    held, sems = refs[6:]
+    pieces = [(i, pl.ds(8 * j, 8)) for j in range(4) for i in range(3)]
+    ins = [
+        pltpu.make_async_copy(refs[i].at[at], held.at[i, at], sems.at[0, n]) for n, (i, at) in enumerate(pieces)
+    ]
+    outs = [
+        pltpu.make_async_copy(held.at[i, at], refs[3 + i].at[at], sems.at[1, n]) for n, (i, at) in enumerate(pieces)
+    ]
+    for copy in ins:
+        copy.start()
+    for first, second in zip(ins, outs):
+        first.wait()
+        second.start()
+    for copy in outs:
+        copy.wait()
 
 
 def body(query_field, key_field, value_field, output_grad):
@@ -607,8 +619,9 @@
     outs = pl.pallas_call(
         copy_kernel,
         out_shape=[jax.ShapeDtypeStruct(flat, F32)] * 3,
-        in_specs=[pl.BlockSpec(memory_space=pltpu.VMEM)] * 3,
-        out_specs=[pl.BlockSpec(memory_space=pltpu.VMEM)] * 3,
+        in_specs=[pl.BlockSpec(memory_space=pl.ANY)] * 3,
+        out_specs=[pl.BlockSpec(memory_space=pl.ANY)] * 3,
+        scratch_shapes=[pltpu.VMEM((3,) + flat, F32), pltpu.SemaphoreType.DMA((2, 12))],
     )(*outs)
     return tuple(x.reshape(frames, rows, cols, channels) for x in outs)
 

time: 62.4 us -> 62.4 us (level)
  no operation moved by 1% of the time
where the time goes in v9:
time: 62.4 us; the launch traced here: 62.1 us
  Pallas kernels  61.4 us (98%)
  between operations  0.64 us (1%)
    pallas_call x1, Pallas kernels, body(): pl.pallas_call(kernel, out_shape=[jax.ShapeDtypeStruct(flat, F32)] * 3, i...  59.7 us
    pallas_call x1, Pallas kernels, body(): pl.pallas_call(copy_kernel, out_shape=[jax.ShapeDtypeStruct(flat, F32)] *...  1.76 us

profile of v9, /device:TPU:14, one launch (start us, length us, event | category | flops | bytes accessed | tf_op | source)
XLA Modules:
  0.0 62.1 jit_solution(17218567872422625263)
XLA Ops:
  0.6 59.7 %shard_map.67 = (f32[32,4,256]{2,1,0:T(4,128)}, f32[32,4,256]{2,1,0:T(4,128)}, f32[32,4,256]{2,1,0:T(4,128)}) custom-call(f32[32,4,256]{2,1,0:T(4,128)} %bitcast.7, f32[32,4,256]{2,1,0:T(4,128)} %bitcast.8, f32[32,4,256]{2,1,0:T(4,128)} %bitcast.9, f32[32,4,256]{2,1,0:T(4,128)} %bitcast.10), custom_call_target="tpu_custom_call" | custom-call | tf_op jit(solution)/shard_map/pallas_call | solution.py:585
  60.3 1.8 %shard_map.68 = (f32[32,4,256]{2,1,0:T(4,128)}, f32[32,4,256]{2,1,0:T(4,128)}, f32[32,4,256]{2,1,0:T(4,128)}) custom-call(f32[32,4,256]{2,1,0:T(4,128)} %get-tuple-element.9.refs_0_, f32[32,4,256]{2,1,0:T(4,128)} %get-tuple-element.10.refs_1_, f32[32,4,256]{2,1,0:T(4,128)} %get-tuple-element.11.refs_2_), custom_call_target="tpu_custom_call" | custom-call | tf_op jit(solution)/shard_map/pallas_call | solution.py:619
